TPU v7x, 128 devices: a whole 4x4x4 slice. The times are simulated.
128 devices in a mesh: role: 2 (over y_lo), grp: 64 (over y_hi, z, x, core).
Axes of the slice: x: 4, y: 4 (y_hi: 2, y_lo: 2; y = y_hi * 2 + y_lo), z: 4, core: 2. Of those that a mesh axis runs over, the one named last changes fastest.
Arguments:
- hidden_state: float32 [128, 8192], P(None, ('role', 'grp')), may hold values from -6 to 6
- gain_attn: float32 [8192], P(('role', 'grp')), may hold values from 0.25 to 1.75
- gain_ffn: float32 [8192], P(('role', 'grp')), may hold values from 0.25 to 1.75
- w_qkv: bfloat16 [9216, 8192], P(('role', 'grp')), may hold values from -0.0625 to 0.0625
- w_out: bfloat16 [8192, 8192], P(('role', 'grp')), may hold values from -0.0625 to 0.0625
- w_gate: bfloat16 [53248, 8192], P(('role', 'grp')), may hold values from -0.0625 to 0.0625
- w_up: bfloat16 [53248, 8192], P(('role', 'grp')), may hold values from -0.0625 to 0.0625
- w_down: bfloat16 [53248, 8192], P(('role', 'grp')), may hold values from -0.02734375 to 0.02734375
- kv_cache: bfloat16 [128, 1024, 1024], P(('role', 'grp'))
- lengths: int32 [128], replicated, may hold values from 1 to 1024, as said below
- row_order: int32 [128], replicated, may hold values from 0 to 127, each once
Outputs:
- out_state: float32 [128, 8192], P(None, ('role', 'grp'))
Inputs may be any that keep to these rules, and one draw needn't show every extreme that they name: `lengths`: every sequence has at least one cached position; some sequence has all 1024. `row_order`: each sequence is named by exactly one cache row.
All inputs are finite; a program needn't handle non-finite values.
Results may differ from a plain program's by a relative error of at most 0.0099.
Values may be sent and summed in bfloat16 or wider, within the bound.
A program may use at most 128 MiB of HBM per device.

v0:
```python
import jax
import jax.numpy as jnp
from jax import lax
from jax.sharding import PartitionSpec as P

QH = 64
KVH = 4
HD = 128


def contract_rows(left, right):
    return lax.dot_general(
        left, right, (((1,), (1,)), ((), ())), preferred_element_type=jnp.float32
    )


def per_device(
    hidden_state,
    gain_attn,
    gain_ffn,
    w_qkv,
    w_out,
    w_gate,
    w_up,
    w_down,
    kv_cache,
    lengths,
    row_order,
):
    place = lax.axis_index("role") * lax.axis_size("grp") + lax.axis_index("grp")
    total_rows = hidden_state.shape[0]
    owned = kv_cache.shape[0]
    length = kv_cache.shape[1]
    key_width = KVH * HD
    query_width = QH * HD
    groups = QH // KVH
    scale = 1.0 / HD**0.5
    inverse = (
        jnp.zeros((total_rows,), jnp.int32)
        .at[row_order]
        .set(jnp.arange(total_rows, dtype=jnp.int32))
    )
    slot_lens = lax.dynamic_slice_in_dim(lengths[row_order], place * owned, owned)
    valid = (jnp.arange(length, dtype=jnp.int32)[None, :] < slot_lens[:, None])[:, None, None, :]
    keys = kv_cache[:, :, :key_width].reshape(owned, length, KVH, HD)
    values = kv_cache[:, :, key_width:].reshape(owned, length, KVH, HD)

    def full_normed(state, gain):
        whole, whole_gain = (
            lax.all_gather(state, ("role", "grp"), axis=1, tiled=True),
            lax.all_gather(gain, ("role", "grp"), axis=0, tiled=True),
        )
        mean = jnp.mean(whole * whole, axis=1, keepdims=True)
        return (whole * lax.rsqrt(mean + 1e-05) * whole_gain).astype(jnp.bfloat16)

    state = hidden_state
    normed_a = full_normed(state, gain_attn)
    projected = contract_rows(normed_a, w_qkv).astype(jnp.bfloat16)
    mine = lax.all_to_all(
        projected[row_order], ("role", "grp"), split_axis=0, concat_axis=1, tiled=True
    )
    recent = [mine[:, query_width:]]
    query = mine[:, :query_width]
    query = query.reshape(owned, KVH, groups, HD)
    fresh_all = jnp.stack(recent, axis=1)
    count = fresh_all.shape[1]
    new_keys = fresh_all[:, :, :key_width].reshape(owned, count, KVH, HD)
    new_values = fresh_all[:, :, key_width:].reshape(owned, count, KVH, HD)
    cached = jnp.einsum("rkgd,rlkd->rkgl", query, keys, preferred_element_type=jnp.float32) * scale
    cached = jnp.where(valid, cached, -1e30)
    fresh = (
        jnp.einsum("rkgd,rjkd->rkgj", query, new_keys, preferred_element_type=jnp.float32) * scale
    )
    top = jnp.maximum(jnp.max(cached, axis=-1), jnp.max(fresh, axis=-1))
    cached_w = jnp.where(valid, jnp.exp(cached - top[..., None]), 0.0)
    fresh_w = jnp.exp(fresh - top[..., None])
    total = jnp.sum(cached_w, axis=-1) + jnp.sum(fresh_w, axis=-1)
    summed = jnp.einsum(
        "rkgl,rlkd->rkgd", cached_w.astype(jnp.bfloat16), values, preferred_element_type=jnp.float32
    )
    summed = summed + jnp.einsum(
        "rkgj,rjkd->rkgd",
        fresh_w.astype(jnp.bfloat16),
        new_values,
        preferred_element_type=jnp.float32,
    )
    attended = (summed / total[..., None]).reshape(owned, query_width).astype(jnp.bfloat16)
    delta = contract_rows(lax.all_gather(attended, ("role", "grp"), axis=0, tiled=True), w_out)
    state = state + delta[inverse]
    normed_f = full_normed(state, gain_ffn)
    gate = contract_rows(normed_f, w_gate)
    upper = contract_rows(normed_f, w_up)
    hidden = (jax.nn.silu(gate) * upper).astype(jnp.bfloat16)
    term = jnp.dot(hidden, w_down, preferred_element_type=jnp.float32)
    summed = lax.psum_scatter(term, ("role", "grp"), scatter_dimension=1, tiled=True)
    state = state + summed
    return state


def solution(mesh):
    in_specs = (
        P(None, ("role", "grp")),
        P(("role", "grp")),
        P(("role", "grp")),
        P(("role", "grp"), None),
        P(("role", "grp"), None),
        P(("role", "grp"), None),
        P(("role", "grp"), None),
        P(("role", "grp"), None),
        P(("role", "grp"), None, None),
        P(),
        P(),
    )
    out_specs = P(None, ("role", "grp"))
    return jax.shard_map(
        per_device, mesh=mesh, in_specs=in_specs, out_specs=out_specs, check_vma=False
    )
```

profile of v0, /device:TPU:1, one launch (start us, length us, event | category | flops | bytes accessed | tf_op | source)
XLA Modules:
  0.0 1441.6 jit_solution(14356021649416771107)
XLA Ops:
  6.5 0.7 all-gather.5.cloned.1.call-update
  7.3 0.9 dynamic-update-slice
  8.2 0.9 dynamic-update-slice.1
  9.7 0.7 compare_select_fusion.1
  10.4 3.0 fusion.31
  13.4 1.2 gather_fusion
  15.3 194.7 %all-gather.5.cloned.1.call-done = f32[128,8192]{0,1:T(8,128)} async-done(((f32[128,64]{0,1:T(8,128)}), f32[128,8192]{0,1:T(8,128)}) %all-gather.5.cloned.1.call-update) | async-done | bytes 4194320 | tf_op jit(solution)/shard_map/all_gather | solution.py:50
  209.9 3.3 multiply_reduce_fusion.1
  213.2 138.9 %all-reduce.5.cloned.1.call-done = (f32[8192]{0:T(1024)}, f32[8192]{0:T(1024)}) async-done(((f32[8192]{0:T(1024)}, f32[8192]{0:T(1024)}), (f32[8192]{0:T(1024)}, f32[8192]{0:T(1024)})) %all-reduce.5.cloned.1.call-update) | async-done | bytes 65552
  352.1 4.9 fusion.9
  357.2 0.7 gather_fusion.1
  357.9 0.7 copy.24
  358.6 5.3 all-to-all-start
  365.2 1.5 copy.38
  366.7 6.9 all-to-all-done
  375.8 1.0 scatter_custom_fusion
  376.9 192.9 %all-gather.9.cloned.1.call-done = bf16[128,1,8192]{2,1,0:T(2,128)(2,1)} async-done(((bf16[1,1,8192]{2,1,0:T(2,128)(2,1)}), bf16[128,1,8192]{2,1,0:T(2,128)(2,1)}) %all-gather.9.cloned.1.call-update) | async-done | bytes 2097168 | tf_op jit(solution)/shard_map/all_gather | solution.py:88
  569.7 4.9 fusion.1
  576.2 196.4 %all-gather.7.cloned.1.call-done = f32[128,8192]{0,1:T(8,128)} async-done(((f32[128,64]{0,1:T(8,128)}), f32[128,8192]{0,1:T(8,128)}) %all-gather.7.cloned.1.call-update) | async-done | bytes 4194320 | tf_op jit(solution)/shard_map/all_gather | solution.py:50
  772.6 3.4 multiply_reduce_fusion
  776.1 5.2 fusion.30
  781.3 15.9 %fusion.11 = f32[128,8192]{0,1:T(8,128)} fusion(bf16[416,8192]{1,0:T(8,128)(2,1)} %param.18, bf16[416,8192]{1,0:T(8,128)(2,1)} %param.17, f32[128,416]{0,1:T(8,128)S(1)} %fusion.30, f32[128,8192]{0,1:T(8,128)} %all-gather.7.cloned.1.call-done, f32[8192]{0:T(1024)S(1)} %copy-done.5, f32[128]{0:T(128)S(1)} %add_rsqrt_fusion), kind=kOutput, calls=%fused_computation.22 | convolution fusion | flops 1748295680 | bytes 22266368 | tf_op jit(solution)/shard_map/dot_general | solution.py:94
  797.3 636.5 %reduce-scatter.2.cloned.1.call-done = f32[128,64]{0,1:T(8,128)} async-done(((f32[128,8192]{0,1:T(8,128)}), f32[128,64]{0,1:T(8,128)}) %reduce-scatter.2.cloned.1.call-update) | async-done | bytes 32784 | tf_op jit(solution)/shard_map/reduce_scatter | solution.py:95
  1433.7 1.4 add.63
  (54 shorter events, 6.6 us)
Async XLA Ops:
  6.5 345.6 %copy-start = (bf16[72,8192]{1,0:T(8,128)(2,1)S(1)}, bf16[72,8192]{1,0:T(8,128)(2,1)}, u32[]{:S(2)}) copy-start(bf16[72,8192]{1,0:T(8,128)(2,1)} %param.14) | copy-start | bytes 3538948
  6.5 6.8 copy-start.1
  6.5 203.4 %all-gather.5.cloned.1.call-start = ((), (), s32[]{:S(2)}) async-start(), calls=%async_computation.2 | async-start | bytes 4227072 | tf_op jit(solution)/shard_map/all_gather | solution.py:50
  7.3 344.9 %all-reduce.5.cloned.1.call-start = ((), (), s32[]{:S(2)}) async-start(), calls=%async_computation.6 | async-start | bytes 131072
  8.2 0.9 copy-start.8
  9.1 0.6 copy-start.7
  15.3 349.3 %copy-start.3 = (bf16[1,1024,512]{2,1,0:T(8,128)(2,1)S(1)}, bf16[1,1024,512]{2,1,0:T(8,128)(2,1)}, u32[]{:S(2)}) copy-start(bf16[1,1024,512]{2,1,0:T(8,128)(2,1)} %get-tuple-element.7) | copy-start | bytes 3145732
  358.6 15.0 %all-to-all-start = ((bf16[128,1,72]{2,1,0:T(2,128)(2,1)}), bf16[128,1,72]{2,1,0:T(2,128)(2,1)S(1)}, u32[]{:S(2)}, u32[]{:S(2)}) async-start(bf16[128,1,72]{2,1,0:T(2,128)(2,1)} %copy.24), calls=%async_computation | async-start | bytes 131072 | tf_op jit(solution)/shard_map/all_to_all | solution.py:59
  363.9 205.8 %all-gather.9.cloned.1.call-start = ((), (), s32[]{:S(2)}) async-start(), calls=%async_computation.5 | async-start | bytes 4227072 | tf_op jit(solution)/shard_map/all_gather | solution.py:88
  366.7 208.7 %copy-start.6 = (f32[128,64]{0,1:T(8,128)S(1)}, f32[128,64]{0,1:T(8,128)}, u32[]{:S(2)}) copy-start(f32[128,64]{0,1:T(8,128)} %param.11) | copy-start | bytes 98308
  375.8 396.8 %all-gather.7.cloned.1.call-start = ((), (), s32[]{:S(2)}) async-start(), calls=%async_computation.3 | async-start | bytes 4227072 | tf_op jit(solution)/shard_map/all_gather | solution.py:50
  376.9 399.2 %copy-start.5 = (f32[8192]{0:T(1024)S(1)}, f32[8192]{0:T(1024)}, u32[]{:S(2)}) copy-start(f32[8192]{0:T(1024)} %get-tuple-element.6) | copy-start | bytes 98308
  576.0 857.7 %reduce-scatter.2.cloned.1.call-start = ((), (), s32[]{:S(2)}) async-start(), calls=%async_computation.4 | async-start | bytes 4227072 | tf_op jit(solution)/shard_map/reduce_scatter | solution.py:95
  772.6 3.4 copy-start.2
  797.2 636.5 %copy-start.4 = (f32[128,64]{0,1:T(8,128)S(1)}, f32[128,64]{0,1:T(8,128)}, u32[]{:S(2)}) copy-start(f32[128,64]{0,1:T(8,128)} %add.60) | copy-start | bytes 98308
Sparse Core Ops, SparseCore 0:
  9.1 200.8 all-gather.4
  214.9 137.1 all-reduce.4
  375.9 193.7 all-gather.8
  576.1 196.4 all-gather.6
  797.4 636.3 reduce-scatter.1
where the time goes:
time: 1460 us; the launch traced here: 1440 us
  waiting for transfers between devices  1370 us (94%)
  matrix products  31.9 us (2%)
    reduce_scatter x1, waiting for transfers between devices, per_device(): lax.psum_scatter(term, ('role', 'grp'), scatter_dimension=1, tiled=True)  636 us
    all_gather x2, waiting for transfers between devices, full_normed(): lax.all_gather(state, ('role', 'grp'), axis=1, tiled=True)  391 us
    all_gather x1, waiting for transfers between devices, per_device(): lax.all_gather(attended, ('role', 'grp'), axis=0, tiled=True)  193 us
    unnamed x6, waiting for transfers between devices  140 us
  transfers between devices with their start and end apart: 6, of which 6 were waited for; matrix products, arithmetic and copies ran while one was open for 1% of the time, Pallas kernels for 0%

commit v1 on v0

v1 whole, which is shorter than its diff:
```python
import jax
import jax.numpy as jnp
from jax import lax
from jax.experimental import pallas as pl
from jax.experimental.pallas import tpu as pltpu
from jax.sharding import PartitionSpec as P

F32 = jnp.float32
BF16 = jnp.bfloat16
D = 8192
QH = 64
KVH = 4
HD = 128
ROWS = 128
DEVICES = 128
FEATURES = D // DEVICES
QKV = (QH + 2 * KVH) * HD // DEVICES
FF = 53248 // DEVICES
CACHE = 1024
EPS = 1e-05
AXES = "yzx"
MESH = pl.DeviceIdType.MESH

PARTS = ((0, 16, "xzy"), (16, 16, "zyx"), (32, 32, "yxz"))
GATHER_SEMS = 13


def iota(shape, dim):
    return lax.broadcasted_iota(jnp.int32, shape, dim)


def dot(a, b, ca=1, cb=0):
    return lax.dot_general(a, b, (((ca,), (cb,)), ((), ())), preferred_element_type=F32)


def kernel(
    hs_ref, ga_ref, gf_ref, len_ref, ord_ref,
    wqkv_hbm, wout_hbm, wg_hbm, wu_hbm, wd_hbm, kv_hbm,
    out_ref,
    wqkv, wout, wg, wu, wd, kv, load_sem,
    xa, sa, xf, sf, a1, fold, att, t_buf, r1, r2,
    pt, rc, rb0, rb1, rb2, fs,
    hid_ref, gate_ref, up_ref,
    xa_send, xa_recv, sa_send, sa_recv, xf_send, xf_recv, sf_send, sf_recv,
    at_send, at_recv, aa_send, aa_recv, rs_send, rs_recv,
):
    role = lax.axis_index("role")
    grp = lax.axis_index("grp")
    c = lax.rem(grp, 2)
    coord = {
        "x": lax.rem(lax.div(grp, 2), 4),
        "z": lax.rem(lax.div(grp, 8), 4),
        "y": role * 2 + lax.div(grp, 32),
    }
    me = role * 64 + grp

    def device(at, core):
        y = at["y"]
        return (lax.div(y, 2), lax.rem(y, 2) * 32 + at["z"] * 8 + at["x"] * 2 + core)

    def shifted(axis, k):
        return {**coord, axis: lax.rem(coord[axis] + k + 4, 4)}

    def peer(axis, k):
        return device(shifted(axis, k), c)

    sibling = device(coord, 1 - c)

    def index(at, full):
        return tuple(slice(None) if a in full else at[a] for a in AXES)

    pending = []

    def send(src, dst, send_sem, recv_sem, target):
        copy = pltpu.make_async_remote_copy(
            src_ref=src, dst_ref=dst, send_sem=send_sem, recv_sem=recv_sem,
            device_id=target, device_id_type=MESH,
        )
        copy.start()
        pending.append(copy)
        return copy

    loads = []
    for i, (src, dst) in enumerate(
        ((wqkv_hbm, wqkv), (kv_hbm, kv), (wout_hbm, wout), (wg_hbm, wg), (wu_hbm, wu), (wd_hbm, wd))
    ):
        load = pltpu.make_async_copy(src, dst, load_sem.at[i])
        load.start()
        loads.append(load)

    others = [sibling]
    for axis in AXES:
        others += [peer(axis, k) for k in (1, 2, 3)]
    for k in (1, 2, 3):
        others.append(device(shifted("x", k), 1 - c))
    for ky in (1, 2, 3):
        for kz in (1, 2, 3):
            others.append(device({**shifted("z", kz), "y": shifted("y", ky)["y"]}, c))
    barrier = pltpu.get_barrier_semaphore()
    for other in others:
        pl.semaphore_signal(barrier, inc=1, device_id=other, device_id_type=MESH)

    def transposed(v):
        return jnp.concatenate([v, jnp.zeros_like(v)], axis=1).T[:FEATURES]

    state = transposed(hs_ref[...])
    gain_f = transposed(jnp.broadcast_to(gf_ref[...], (ROWS, FEATURES)))
    gain_a = transposed(jnp.broadcast_to(ga_ref[...], (ROWS, FEATURES)))
    own = tuple(coord[a] for a in AXES)
    xa[own + (c,)] = (state * gain_a).astype(BF16)
    sa[own + (c,)] = jnp.sum(state * state, axis=0, keepdims=True)

    order_row = ord_ref[...]
    by_seq = (iota((ROWS, ROWS), 0) == order_row).astype(F32)
    by_slot = by_seq.T.astype(BF16)
    lane = iota((1, ROWS), 1)
    my_seq = jnp.sum(jnp.where(lane == me, order_row, 0), axis=1, keepdims=True)
    my_len = jnp.sum(jnp.where(lane == my_seq, len_ref[...], 0), axis=1, keepdims=True)

    pl.semaphore_wait(barrier, len(others))

    class Gather:
        def __init__(self, buf, order, tail, send_sem, recv_sem, base, cored=True):
            self.buf, self.order, self.tail = buf, order, tail
            self.send_sem, self.recv_sem, self.base = send_sem, recv_sem, base
            self.copies = [[], [], [], []]

        def go(self, stage, sem, where, target):
            ref = self.buf.at[where + (c,) + self.tail]
            sem = self.base + sem
            self.copies[stage].append(
                send(ref, ref, self.send_sem.at[sem], self.recv_sem.at[sem], target)
            )

        def step(self, stage):
            if stage:
                for copy in self.copies[stage - 1]:
                    copy.wait_recv()
            where = index(coord, self.order[:stage])
            for k in (2, 1, 3):
                self.go(stage, stage * 3 + k - 1, where, peer(self.order[stage], k))
            if stage == 2:
                self.go(3, 9, where, sibling)

        def last(self, k):
            self.copies[2][(2, 1, 3).index(k)].wait_recv()
            where = index(shifted(self.order[2], -k), self.order[:2])
            self.go(3, 9 + k, where, sibling)

        def finish(self):
            for copy in self.copies[3]:
                copy.wait_recv()

    def run_gather(gathers):
        for stage in range(3):
            for g in gathers:
                g.step(stage)
        for k in (1, 3, 2):
            for g in gathers:
                g.last(k)
        for g in gathers:
            g.finish()

    def state_gather(x, s, x_send, x_recv, s_send, s_recv):
        gathers = [Gather(s, "xzy", (), s_send, s_recv, 0)]
        for p, (at, n, order) in enumerate(PARTS):
            gathers.append(Gather(x, order, (pl.ds(at, n),), x_send, x_recv, p * GATHER_SEMS))
        run_gather(gathers)

    def row_scale(s):
        total = jnp.sum(s[...].reshape(DEVICES, ROWS), axis=0, keepdims=True)
        return lax.rsqrt(total * (1.0 / D) + EPS)

    state_gather(xa, sa, xa_send, xa_recv, sa_send, sa_recv)
    loads[0].wait()
    proj = jnp.zeros((QKV, ROWS), F32)
    for y in range(4):
        block = xa[y].reshape(D // 4, ROWS)
        proj = proj + dot(wqkv[:, y * (D // 4):(y + 1) * (D // 4)], block)
    proj = (proj * row_scale(sa)).astype(BF16)

    lane_of = lax.rem(me * QKV + iota((QKV, HD), 0), HD)
    place = (lane_of == iota((QKV, HD), 1)).astype(BF16)
    placed = dot(proj, place, 0, 0).astype(BF16)
    t_buf[...] = dot(by_slot, placed).reshape(16, 8, 1, HD)
    xc = coord["x"] * 2 + c
    yz = coord["y"] * 4 + coord["z"]
    first, second = [], []
    n = 0
    for kx in range(4):
        for kc in range(2):
            if kx or kc:
                at, core = shifted("x", kx), lax.rem(c + kc, 2)
                first.append(send(t_buf.at[:, at["x"] * 2 + core], r1.at[xc],
                                  aa_send.at[n], aa_recv.at[n], device(at, core)))
                n += 1
    r1[xc] = t_buf[:, xc]
    for copy in first:
        copy.wait_recv()
    for ky in range(4):
        for kz in range(4):
            if ky or kz:
                at = {**shifted("z", kz), "y": shifted("y", ky)["y"]}
                second.append(send(r1.at[:, at["y"] * 4 + at["z"]], r2.at[yz],
                                   aa_send.at[n], aa_recv.at[n], device(at, c)))
                n += 1
    r2[yz] = r1[:, yz]
    for copy in second:
        copy.wait_recv()
    got = r2[...].reshape(DEVICES, HD)
    start = iota((DEVICES, HD), 0) * QKV
    late = iota((DEVICES, HD), 1) >= lax.rem(start, HD)
    heads = QH + 2 * KVH
    src_head = lax.div(iota((heads, DEVICES), 1) * QKV, HD)
    head = iota((heads, DEVICES), 0)
    qkv = dot((src_head == head).astype(BF16), jnp.where(late, got, 0.0).astype(BF16))
    qkv = qkv + dot((src_head + 1 == head).astype(BF16), jnp.where(late, 0.0, got).astype(BF16))

    loads[1].wait()
    groups = QH // KVH
    valid = iota((groups, CACHE), 1) < my_len
    outs = []
    for h in range(KVH):
        q = qkv[h * groups:(h + 1) * groups]
        k_new = qkv[QH + h:QH + h + 1]
        v_new = qkv[QH + KVH + h:QH + KVH + h + 1]
        keys = kv[0, :, h * HD:(h + 1) * HD]
        values = kv[0, :, (KVH + h) * HD:(KVH + h + 1) * HD]
        cached = jnp.where(valid, dot(q.astype(BF16), keys, 1, 1) * (1.0 / HD ** 0.5), -1e30)
        fresh = jnp.sum(q * k_new, axis=1, keepdims=True) * (1.0 / HD ** 0.5)
        top = jnp.maximum(jnp.max(cached, axis=1, keepdims=True), fresh)
        cached_w = jnp.where(valid, jnp.exp(cached - top), 0.0)
        fresh_w = jnp.exp(fresh - top)
        total = jnp.sum(cached_w, axis=1, keepdims=True) + fresh_w
        summed = dot(cached_w.astype(BF16), values) + fresh_w.astype(BF16).astype(F32) * v_new
        outs.append((summed / total).astype(BF16))
    a1[own] = jnp.concatenate(outs, axis=0)

    def plane_step(p, stage, done):
        at, n, order = PARTS[p]
        for copy in done:
            copy.wait_recv()
        ref = a1.at[index(coord, order[:stage]) + (pl.ds(at, n),)]
        sems = [p * GATHER_SEMS + stage * 3 + k - 1 for k in (1, 2, 3)]
        return [send(ref, ref, at_send.at[s], at_recv.at[s], peer(order[stage], k))
                for k, s in zip((1, 2, 3), sems)]

    def att_ref(p, where):
        at, n, order = PARTS[p]
        return att.at[pl.ds(at, n), where[order[2]] * 2 + c]

    stages = [[] for _ in PARTS]
    for stage in range(2):
        for p in range(len(PARTS)):
            stages[p] = plane_step(p, stage, stages[p])
    to_sibling = [[] for _ in PARTS]
    for p, (at, n, order) in enumerate(PARTS):
        for copy in stages[p]:
            copy.wait_recv()
        plane = a1[index(coord, order[:2]) + (slice(at, at + n),)].reshape(16 * n, HD)
        fold[0:16 * n] = plane.astype(F32)
        rows = [fold[pl.ds(h, 16, stride=n)] for h in range(n)]
        att[pl.ds(at, n), coord[order[2]] * 2 + c] = jnp.stack(rows).astype(BF16)
        stages[p] = []
        for k in (1, 2, 3):
            s = p * GATHER_SEMS + 6 + k - 1
            ref = att_ref(p, coord)
            stages[p].append(send(ref, ref, at_send.at[s], at_recv.at[s], peer(order[2], k)))
        s = p * GATHER_SEMS + 9
        ref = att_ref(p, coord)
        to_sibling[p].append(send(ref, ref, at_send.at[s], at_recv.at[s], sibling))
    for k in (1, 3, 2):
        for p, (at, n, order) in enumerate(PARTS):
            stages[p][k - 1].wait_recv()
            s = p * GATHER_SEMS + 9 + k
            ref = att_ref(p, shifted(order[2], -k))
            to_sibling[p].append(send(ref, ref, at_send.at[s], at_recv.at[s], sibling))
    loads[2].wait()
    for p, (at, n, order) in enumerate(PARTS):
        for copy in to_sibling[p]:
            copy.wait_recv()
        block = jnp.concatenate([att[h].reshape(ROWS, HD) for h in range(at, at + n)], axis=1)
        delta = dot(wout[:, at * HD:(at + n) * HD], block, 1, 1)
        j = iota((ROWS, ROWS), 0)
        rest = sorted(order[:2], key=AXES.index)
        digits = {order[2]: lax.div(j, 32), rest[0]: lax.rem(lax.div(j, 4), 4), rest[1]: lax.rem(j, 4)}
        slot = ((digits["y"] * 4 + digits["z"]) * 4 + digits["x"]) * 2 + lax.rem(lax.div(j, 16), 2)
        to_seq = dot((slot == iota((ROWS, ROWS), 1)).astype(BF16), by_slot).astype(BF16)
        for _ in range(3):
            term = delta.astype(BF16)
            state = state + dot(term, to_seq)
            delta = delta - term.astype(F32)

    xf[own + (c,)] = (state * gain_f).astype(BF16)
    sf[own + (c,)] = jnp.sum(state * state, axis=0, keepdims=True)
    state_gather(xf, sf, xf_send, xf_recv, sf_send, sf_recv)
    loads[3].wait()
    loads[4].wait()
    for w, acc in ((wg, gate_ref), (wu, up_ref)):
        for y in range(4):
            block = xf[y].reshape(D // 4, ROWS)
            term = dot(w[:, y * (D // 4):(y + 1) * (D // 4)], block)
            acc[...] = term if y == 0 else acc[...] + term
    scale = row_scale(sf)
    gate = gate_ref[...] * scale
    hidden = gate / (1.0 + jnp.exp(-gate)) * (up_ref[...] * scale)
    hid_ref[...] = hidden.T.astype(BF16)

    loads[5].wait()
    half = ROWS // 2
    core_copies = []
    for y in range(4):
        def chunk(z, carry, y=y):
            lanes = pl.ds(pl.multiple_of((y * 4 + z) * 512, 512), 512)
            term = dot(hid_ref[...], wd[:, lanes]).astype(BF16)
            for x in range(4):
                block = term[:, x * 128:(x + 1) * 128]
                pt[y, z, x, 0] = block[:half]
                pt[y, z, x, 1] = block[half:]
            return carry

        lax.fori_loop(0, 4, chunk, 0)
        core_copies.append(send(pt.at[y, :, :, 1 - c], rc.at[y], rs_send.at[y], rs_recv.at[y], sibling))
    for y in range(4):
        core_copies[y].wait_recv()
        pt[y, :, :, c] = (pt[y, :, :, c].astype(F32) + rc[y].astype(F32)).astype(BF16)

    arrivals = [[] for _ in PARTS]

    def reduced(p, stage):
        at, n, order = PARTS[p]
        rows = (pl.ds(at, n),)
        land = (rb0, rb1, rb2)[stage - 1]
        value = pt[index(coord, order[stage:]) + (c,) + rows].astype(F32)
        for k, copy in enumerate(arrivals[p]):
            copy.wait_recv()
            value = value + land[(k,) + (slice(None),) * (3 - stage) + rows].astype(F32)
        return value

    for stage in range(3):
        for p, (at, n, order) in enumerate(PARTS):
            rows = (pl.ds(at, n),)
            if stage:
                pt[index(coord, order[stage:]) + (c,) + rows] = reduced(p, stage).astype(BF16)
            arrivals[p] = []
            land = (rb0, rb1, rb2)[stage]
            for k in (1, 2, 3):
                src = pt.at[index(shifted(order[stage], k), order[stage + 1:]) + (c,) + rows]
                dst = land.at[(k - 1,) + (slice(None),) * (2 - stage) + rows]
                s = 4 + p * 9 + stage * 3 + k - 1
                arrivals[p].append(send(src, dst, rs_send.at[s], rs_recv.at[s], peer(order[stage], k)))
    for p, (at, n, order) in enumerate(PARTS):
        fs[c, pl.ds(at, n)] = reduced(p, 3)
    s = 4 + 9 * len(PARTS)
    copy = send(fs.at[c], fs.at[c], rs_send.at[s], rs_recv.at[s], sibling)
    copy.wait_recv()
    summed = fs[...].reshape(ROWS, 2 * FEATURES)
    summed = jnp.where(c == 0, summed[:, :FEATURES], summed[:, FEATURES:])
    state = jnp.concatenate([state, jnp.zeros_like(state)], axis=0).T[:, :FEATURES]
    out_ref[...] = state + summed
    for copy in pending:
        copy.wait_send()


def per_device(
    hidden_state, gain_attn, gain_ffn, w_qkv, w_out, w_gate, w_up, w_down, kv_cache, lengths, row_order
):
    parts = len(PARTS)
    vmem = pltpu.VMEM
    dma = pltpu.SemaphoreType.DMA
    scratch = [
        vmem((QKV, D), BF16), vmem((FEATURES, D), BF16), vmem((FF, D), BF16), vmem((FF, D), BF16),
        vmem((FF, D), BF16), vmem((1, CACHE, 2 * KVH * HD), BF16), dma((6,)),
        vmem((4, 4, 4, 2, FEATURES, ROWS), BF16), vmem((4, 4, 4, 2, 1, ROWS), F32),
        vmem((4, 4, 4, 2, FEATURES, ROWS), BF16), vmem((4, 4, 4, 2, 1, ROWS), F32),
        vmem((4, 4, 4, QH, HD), BF16), vmem((16 * 32, HD), F32), vmem((QH, 8, 16, HD), BF16),
        vmem((16, 8, 1, HD), F32), vmem((8, 16, 1, HD), F32), vmem((16, 8, 1, HD), F32),
        vmem((4, 4, 4, 2, ROWS // 2, 128), BF16), vmem((4, 4, 4, ROWS // 2, 128), BF16),
        vmem((3, 4, 4, ROWS // 2, 128), BF16), vmem((3, 4, ROWS // 2, 128), BF16),
        vmem((3, ROWS // 2, 128), BF16), vmem((2, ROWS // 2, 128), F32),
        vmem((ROWS, FF), BF16), vmem((FF, ROWS), F32), vmem((FF, ROWS), F32),
    ]
    for count in (parts * GATHER_SEMS, GATHER_SEMS, parts * GATHER_SEMS, GATHER_SEMS,
                  parts * GATHER_SEMS, 22, 5 + 9 * parts):
        scratch += [dma((count,)), dma((count,))]
    in_vmem = pl.BlockSpec(memory_space=pltpu.VMEM)
    anywhere = pl.BlockSpec(memory_space=pl.ANY)
    return pl.pallas_call(
        kernel,
        out_shape=jax.ShapeDtypeStruct((ROWS, FEATURES), F32),
        in_specs=[in_vmem] * 5 + [anywhere] * 6,
        out_specs=in_vmem,
        scratch_shapes=scratch,
        compiler_params=pltpu.CompilerParams(
            collective_id=0, has_side_effects=True, vmem_limit_bytes=56 * 1024 * 1024
        ),
    )(
        hidden_state, gain_attn.reshape(1, FEATURES), gain_ffn.reshape(1, FEATURES),
        lengths.reshape(1, ROWS), row_order.reshape(1, ROWS),
        w_qkv, w_out, w_gate, w_up, w_down, kv_cache,
    )


def solution(mesh):
    both = ("role", "grp")
    in_specs = (
        P(None, both), P(both), P(both), P(both, None), P(both, None), P(both, None),
        P(both, None), P(both, None), P(both, None, None), P(), P(),
    )
    return jax.shard_map(
        per_device, mesh=mesh, in_specs=in_specs, out_specs=P(None, both), check_vma=False
    )
```

time: 1460 us -> 103 us (0.07); the launches traced: 1440 us -> 103 us
  waiting for transfers between devices: 1370 us -> 0 us
  Pallas kernels: 0 us -> 99.8 us
  matrix products: 31.9 us -> 0 us
    reduce_scatter x1 -> x0, waiting for transfers between devices: 636 us -> none  [per_device(): lax.psum_scatter(term, ('role', 'grp'), scatter_dimension=1, tiled=True)]
    all_gather x3 -> x0, waiting for transfers between devices: 584 us -> none  [the longest x2 391 us: full_normed(): lax.all_gather(state, ('role', 'grp'), axis=1, tiled=True)]
    unnamed x6 -> x0, waiting for transfers between devices: 140 us -> none
    pallas_call x0 -> x1, Pallas kernels: none -> 99.8 us  [per_device(): pl.pallas_call(kernel, out_shape=jax.ShapeDtypeStruct((ROWS, FEATURES), F...]
    dot_general x7 -> x0, matrix products: 31.9 us -> none  [the longest x1 15.9 us: per_device(): term = jnp.dot(hidden, w_down, preferred_element_type=jnp.float32)]
  transfers between devices with their start and end apart: 6 -> 0, of which waited for: 6 -> 0; matrix products, arithmetic and copies ran while one was open for 1% -> 0% of each run, Pallas kernels for 0% -> 0%
where the time goes in v1:
time: 103 us
  Pallas kernels  99.8 us (97%)
  local copies, waits for them, and re-layouts  3.01 us (3%)
    pallas_call x1, Pallas kernels, per_device(): pl.pallas_call(kernel, out_shape=jax.ShapeDtypeStruct((ROWS, FEATURES), F...  99.8 us

profile of v1, /device:TPU:1, one launch (start us, length us, event | category | flops | bytes accessed | tf_op | source)
XLA Modules:
  0.0 102.8 jit_solution(12786342561380036425)
XLA Ops:
  0.0 1.5 %copy.12.hs_ref = f32[128,64]{1,0:T(8,128)} copy(f32[128,64]{0,1:T(8,128)} %param.11) | data formatting | bytes 65536 | tf_op args[0]
  1.5 99.8 %shard_map.109 = f32[128,64]{1,0:T(8,128)} custom-call(f32[128,64]{1,0:T(8,128)} %copy.12.hs_ref, f32[1,64]{1,0:T(1,128)} %bitcast.4, f32[1,64]{1,0:T(1,128)} %bitcast.5, s32[1,128]{1,0:T(1,128)} %bitcast.6, s32[1,128]{1,0:T(1,128)} %bitcast.7, bf16[72,8192]{1,0:T(8,128)(2,1)} %wqkv_hbm.1, bf16[64,8192]{1,0:T(8,128)(2,1)} %wout_hbm.1, ...), custom_call_target="tpu_custom_call" | custom-call | tf_op jit(solution)/shard_map/pallas_call | solution.py:388
  101.2 1.5 %copy.13 = f32[128,64]{0,1:T(8,128)} copy(f32[128,64]{1,0:T(8,128)} %shard_map.109) | data formatting | bytes 65536 | tf_op jit(solution)/shard_map/pallas_call | solution.py:388

commit v2 on v1

v2 whole, which is shorter than its diff:
```python
import jax
import jax.numpy as jnp
from jax import lax
from jax.experimental import pallas as pl
from jax.experimental.pallas import tpu as pltpu
from jax.sharding import PartitionSpec as P

F32 = jnp.float32
BF16 = jnp.bfloat16
D = 8192
QH = 64
KVH = 4
HD = 128
ROWS = 128
DEVICES = 128
FOLD = QH + 8
FEATURES = D // DEVICES
QKV = (QH + 2 * KVH) * HD // DEVICES
FF = 53248 // DEVICES
CACHE = 1024
EPS = 1e-05
AXES = "yzx"
MESH = pl.DeviceIdType.MESH

PARTS = ((0, 16, "x"), (16, 16, "z"), (32, 32, "y"))
OFFSETS = sorted(((i, j) for i in range(4) for j in range(4) if i or j),
                 key=lambda o: -sum(min(k, 4 - k) for k in o))


def iota(shape, dim):
    return lax.broadcasted_iota(jnp.int32, shape, dim)


def dot(a, b, ca=1, cb=0):
    return lax.dot_general(a, b, (((ca,), (cb,)), ((), ())), preferred_element_type=F32)


def kernel(
    hs_hbm, ga_ref, gf_ref, len_ref, ord_ref,
    wqkv_hbm, wout_hbm, wg_hbm, wu_hbm, wd_hbm, kv_hbm,
    out_ref,
    wqkv, wout, wg, wu, wd, kv, load_sem,
    hs, xa, sa, xf, sf, xt, f0, f1, f2, f3, att, t_buf, r1, r2,
    pt, rc, rb0, rb1, fs,
    hid_ref, gate_ref, up_ref,
    xa_send, xa_recv, sa_send, sa_recv, xf_send, xf_recv, sf_send, sf_recv,
    xt_send, xt_recv, aa_send, aa_recv, rs_send, rs_recv,
):
    role = lax.axis_index("role")
    grp = lax.axis_index("grp")
    c = lax.rem(grp, 2)
    coord = {
        "x": lax.rem(lax.div(grp, 2), 4),
        "z": lax.rem(lax.div(grp, 8), 4),
        "y": lax.div(grp, 32) * 2 + role,
    }
    me = role * 64 + grp

    def place_of(axis, value):
        return lax.rem(value, 2) * 2 + lax.div(value, 2) if axis == "y" else value

    def device(at, core):
        y = at["y"]
        return (lax.rem(y, 2), lax.div(y, 2) * 32 + at["z"] * 8 + at["x"] * 2 + core)

    def shifted(axis, k):
        return moved((axis,), (k,))

    def peer(axis, k):
        return device(shifted(axis, k), c)

    sibling = device(coord, 1 - c)

    def index(at, full=""):
        return tuple(slice(None) if a in full else place_of(a, at[a]) for a in AXES)

    def plane_of(axis):
        return AXES.replace(axis, "")

    def moved(axes, offsets):
        return {**coord, **{a: lax.rem(coord[a] + k + 4, 4) for a, k in zip(axes, offsets)}}

    def wait(ref, sem):
        pltpu.make_async_copy(ref, ref, sem).wait()

    pending = []

    def send(src, dst, send_sem, recv_sem, target):
        copy = pltpu.make_async_remote_copy(
            src_ref=src, dst_ref=dst, send_sem=send_sem, recv_sem=recv_sem,
            device_id=target, device_id_type=MESH,
        )
        copy.start()
        pending.append(copy)
        return copy

    loads = []
    for i, (src, dst) in enumerate(
        ((hs_hbm, hs), (wqkv_hbm, wqkv), (kv_hbm, kv), (wout_hbm, wout), (wg_hbm, wg), (wu_hbm, wu), (wd_hbm, wd))
    ):
        load = pltpu.make_async_copy(src, dst, load_sem.at[i])
        load.start()
        loads.append(load)

    others = [sibling]
    for axis in AXES:
        others += [device(moved(plane_of(axis), o), c) for o in OFFSETS if 0 not in o]
        others += [peer(axis, k) for k in (1, 2, 3)]
    for k in (1, 2, 3):
        others.append(device(shifted("x", k), 1 - c))
    barrier = pltpu.get_barrier_semaphore()
    for other in others:
        pl.semaphore_signal(barrier, inc=1, device_id=other, device_id_type=MESH)

    def transposed(v):
        return jnp.concatenate([v, jnp.zeros_like(v)], axis=1).T[:FEATURES]

    gain_f = transposed(jnp.broadcast_to(gf_ref[...], (ROWS, FEATURES)))
    gain_a = transposed(jnp.broadcast_to(ga_ref[...], (ROWS, FEATURES)))
    own = index(coord)
    loads[0].wait()
    state = transposed(hs[...])
    xa[own + (c,)] = (state * gain_a).astype(BF16)
    sa[own + (c,)] = jnp.sum(state * state, axis=0, keepdims=True)

    order_row = ord_ref[...]
    by_seq = (iota((ROWS, ROWS), 0) == order_row).astype(F32)
    by_slot = by_seq.T.astype(BF16)
    lane = iota((1, ROWS), 1)
    my_seq = jnp.sum(jnp.where(lane == me, order_row, 0), axis=1, keepdims=True)
    my_len = jnp.sum(jnp.where(lane == my_seq, len_ref[...], 0), axis=1, keepdims=True)

    pl.semaphore_wait(barrier, len(others))

    class Gather:
        def __init__(self, buf, axis, tail, send_sem, recv_sem, base):
            self.buf, self.axis, self.tail = buf, axis, tail
            self.plane = plane_of(axis)
            self.send_sem, self.recv_sem, self.base = send_sem.at[base], recv_sem, base * 12

        def at(self, where):
            return self.buf.at[where + (c,) + self.tail]

        def sem(self, stage, row):
            return self.recv_sem.at[self.base + stage * 4 + row]

        def row(self, k):
            return index(moved(self.plane[:1], (k,)), self.plane[1:])

        def push(self, ref, sem, target):
            pltpu.make_async_remote_copy(
                src_ref=ref, dst_ref=ref, send_sem=self.send_sem, recv_sem=sem,
                device_id=target, device_id_type=MESH,
            ).start()

        def spread(self, offset):
            sem = self.sem(0, (4 - offset[0]) % 4)
            self.push(self.at(own), sem, device(moved(self.plane, offset), c))

        def forward(self, k):
            where = self.row(k)
            some = tuple(pl.ds(0, 3) if a == self.plane[1] and k == 0 else w for a, w in zip(AXES, where))
            wait(self.at(some), self.sem(0, k))
            for j in (2, 1, 3):
                self.push(self.at(where), self.sem(1, k), peer(self.axis, j))

        def share(self, k):
            where = self.row(k)
            wait(self.at(tuple(pl.ds(0, 3) if a == self.axis else w for a, w in zip(AXES, where))), self.sem(1, k))
            where = tuple(slice(None) if a == self.axis else w for a, w in zip(AXES, where))
            self.push(self.at(where), self.sem(2, k), sibling)

        def finish(self, k):
            where = tuple(slice(None) if a == self.axis else w for a, w in zip(AXES, self.row(k)))
            wait(self.buf.at[where + (1 - c,) + self.tail], self.sem(2, k))

        def sent(self):
            blocks = self.buf.reshape(DEVICES, *self.buf.shape[4:])
            wait(blocks.at[(pl.ds(0, 127),) + self.tail], self.send_sem)

    gathered = []

    def gather(x, x_send, x_recv, s=None, s_send=None, s_recv=None):
        runs = [] if s is None else [Gather(s, "x", (), s_send, s_recv, 0)]
        for p, (at, n, axis) in enumerate(PARTS):
            runs.append(Gather(x, axis, (pl.ds(at, n),), x_send, x_recv, p))
        for offset in OFFSETS:
            for run in runs:
                run.spread(offset)
        for step in ("forward", "share", "finish"):
            for k in (0, 1, 3, 2):
                for run in runs:
                    getattr(run, step)(k)
        gathered.extend(runs)

    def row_scale(s):
        total = jnp.sum(s[...].reshape(DEVICES, ROWS), axis=0, keepdims=True)
        return lax.rsqrt(total * (1.0 / D) + EPS)

    gather(xa, xa_send, xa_recv, sa, sa_send, sa_recv)
    loads[1].wait()
    proj = jnp.zeros((QKV, ROWS), F32)
    for y in range(4):
        block = xa[y].reshape(D // 4, ROWS)
        proj = proj + dot(wqkv[:, y * (D // 4):(y + 1) * (D // 4)], block)
    proj = (proj * row_scale(sa)).astype(BF16)

    lane_of = lax.rem(me * QKV + iota((QKV, HD), 0), HD)
    place = (lane_of == iota((QKV, HD), 1)).astype(BF16)
    placed = dot(proj, place, 0, 0).astype(BF16)
    t_buf[...] = dot(by_slot, placed).reshape(16, 8, 1, HD)
    xc = coord["x"] * 2 + c
    yz = place_of("y", coord["y"]) * 4 + coord["z"]
    first, second = [], []
    n = 0
    for kx in range(4):
        for kc in range(2):
            if kx or kc:
                at, core = shifted("x", kx), lax.rem(c + kc, 2)
                first.append(send(t_buf.at[:, at["x"] * 2 + core], r1.at[xc],
                                  aa_send.at[n], aa_recv.at[n], device(at, core)))
                n += 1
    r1[xc] = t_buf[:, xc]
    for copy in first:
        copy.wait_recv()
    for o in OFFSETS:
        at = moved("yz", o)
        second.append(send(r1.at[:, place_of("y", at["y"]) * 4 + at["z"]], r2.at[yz],
                           aa_send.at[n], aa_recv.at[n], device(at, c)))
        n += 1
    r2[yz] = r1[:, yz]
    for copy in second:
        copy.wait_recv()
    got = r2[...].reshape(DEVICES, HD)
    start = iota((DEVICES, HD), 0) * QKV
    late = iota((DEVICES, HD), 1) >= lax.rem(start, HD)
    heads = QH + 2 * KVH
    src_head = lax.div(iota((heads, DEVICES), 1) * QKV, HD)
    head = iota((heads, DEVICES), 0)
    qkv = dot((src_head == head).astype(BF16), jnp.where(late, got, 0.0).astype(BF16))
    qkv = qkv + dot((src_head + 1 == head).astype(BF16), jnp.where(late, 0.0, got).astype(BF16))

    loads[2].wait()
    groups = QH // KVH
    valid = iota((groups, CACHE), 1) < my_len
    outs = []
    for h in range(KVH):
        q = qkv[h * groups:(h + 1) * groups]
        k_new = qkv[QH + h:QH + h + 1]
        v_new = qkv[QH + KVH + h:QH + KVH + h + 1]
        keys = kv[0, :, h * HD:(h + 1) * HD]
        values = kv[0, :, (KVH + h) * HD:(KVH + h + 1) * HD]
        cached = jnp.where(valid, dot(q.astype(BF16), keys, 1, 1) * (1.0 / HD ** 0.5), -1e30)
        fresh = jnp.sum(q * k_new, axis=1, keepdims=True) * (1.0 / HD ** 0.5)
        top = jnp.maximum(jnp.max(cached, axis=1, keepdims=True), fresh)
        cached_w = jnp.where(valid, jnp.exp(cached - top), 0.0)
        fresh_w = jnp.exp(fresh - top)
        total = jnp.sum(cached_w, axis=1, keepdims=True) + fresh_w
        summed = dot(cached_w.astype(BF16), values) + fresh_w.astype(BF16).astype(F32) * v_new
        outs.append((summed / total).astype(BF16))
    xt[own + (c,)] = jnp.concatenate(outs, axis=0)

    gather(xt, xt_send, xt_recv)
    loads[3].wait()
    for y, fold in enumerate((f0, f1, f2, f3)):
        slots = ROWS // 4
        for i in range(slots):
            fold[i * FOLD:i * FOLD + QH] = xt[y, i // 8, i // 2 % 4, i % 2].astype(F32)
        for h in range(QH):
            att[h, y * slots:(y + 1) * slots] = fold[pl.ds(h, slots, stride=FOLD)].astype(BF16)
    delta = jnp.zeros((FEATURES, ROWS), F32)
    for h in range(0, QH, 16):
        block = jnp.concatenate([att[i] for i in range(h, h + 16)], axis=1)
        delta = delta + dot(wout[:, h * HD:(h + 16) * HD], block, 1, 1)
    for _ in range(3):
        term = delta.astype(BF16)
        state = state + dot(term, by_slot)
        delta = delta - term.astype(F32)

    xf[own + (c,)] = (state * gain_f).astype(BF16)
    sf[own + (c,)] = jnp.sum(state * state, axis=0, keepdims=True)
    gather(xf, xf_send, xf_recv, sf, sf_send, sf_recv)
    loads[4].wait()
    loads[5].wait()
    for w, acc in ((wg, gate_ref), (wu, up_ref)):
        for y in range(4):
            block = xf[y].reshape(D // 4, ROWS)
            term = dot(w[:, y * (D // 4):(y + 1) * (D // 4)], block)
            acc[...] = term if y == 0 else acc[...] + term
    scale = row_scale(sf)
    gate = gate_ref[...] * scale
    hidden = gate / (1.0 + jnp.exp(-gate)) * (up_ref[...] * scale)
    hid_ref[...] = hidden.T.astype(BF16)

    loads[6].wait()
    half = ROWS // 2
    slabs = (2, 1, 3, 0)
    lines = (slice(None),) * 2

    def push(src, dst, send_sem, recv_sem, target):
        pltpu.make_async_remote_copy(
            src_ref=src, dst_ref=dst, send_sem=send_sem, recv_sem=recv_sem,
            device_id=target, device_id_type=MESH,
        ).start()

    def slab_of(k):
        return place_of("y", moved("y", (k,))["y"])

    def down(k):
        y = slab_of(k)

        def chunk(z, carry):
            lanes = pl.ds(pl.multiple_of((y * 4 + z) * 512, 512), 512)
            term = dot(hid_ref[...], wd[:, lanes]).astype(BF16)
            for x in range(4):
                block = term[:, x * 128:(x + 1) * 128]
                pt[y, z, x, 0] = block[:half]
                pt[y, z, x, 1] = block[half:]
            return carry

        lax.fori_loop(0, 4, chunk, 0)
        push(pt.at[y, :, :, 1 - c], rc.at[y], rs_send.at[0], rs_recv.at[k], sibling)

    def along(k):
        y = slab_of(k)
        wait(rc.at[y], rs_recv.at[k])
        pt[y, :, :, c] = (pt[y, :, :, c].astype(F32) + rc[y].astype(F32)).astype(BF16)
        for p, (at, n, axis) in enumerate(PARTS):
            rows = pl.ds(at, n)
            if axis == "y":
                if k:
                    push(pt.at[y, :, :, c, rows], rb0.at[k - 1, :, :, rows],
                         rs_send.at[1 + p], rs_recv.at[4 + p * 5], peer("y", k))
                continue
            for j in (2, 1, 3):
                where = index({**shifted(axis, j), "y": moved("y", (k,))["y"]}, plane_of(axis)[1:])
                push(pt.at[where + (c, rows)], rb0.at[j - 1, y, :, rows],
                     rs_send.at[1 + p], rs_recv.at[4 + p * 5 + k], peer(axis, j))

    def across(p, line, where, sem, offsets):
        at, n, axis = PARTS[p]
        rows = pl.ds(at, n)
        wait(rb0.at[(slice(None),) + line + (rows,)], rs_recv.at[sem])
        value = pt[where + (c, rows)].astype(F32)
        for j in range(3):
            value = value + rb0[(j,) + line + (rows,)].astype(F32)
        pt[where + (c, rows)] = value.astype(BF16)
        for o in offsets:
            target = moved(plane_of(axis), o)
            push(pt.at[index(target) + (c, rows)], rb1.at[o[0] * 4 + o[1], rows],
                 rs_send.at[1 + p], rs_recv.at[4 + p * 5 + 4], device(target, c))

    down(slabs[0])
    for i, k in enumerate(slabs):
        if i < 3:
            down(slabs[i + 1])
        along(k)
    for k in slabs:
        for p, (at, n, axis) in enumerate(PARTS):
            if axis == "y":
                if k == 0:
                    across(p, lines, index(coord, plane_of("y")), 4 + p * 5, OFFSETS)
            else:
                where = index(moved("y", (k,)), plane_of(axis)[1:])
                across(p, (slab_of(k), slice(None)), where, 4 + p * 5 + k,
                       [o for o in OFFSETS if o[0] == k])
    for p, (at, n, axis) in enumerate(PARTS):
        rows = pl.ds(at, n)
        wait(rb1.at[pl.ds(1, 15), rows], rs_recv.at[4 + p * 5 + 4])
        value = pt[own + (c, rows)].astype(F32)
        for i in range(1, 16):
            value = value + rb1[i, rows].astype(F32)
        fs[c, rows] = value
    push(fs.at[c], fs.at[c], rs_send.at[4], rs_recv.at[19], sibling)
    wait(fs.at[1 - c], rs_recv.at[19])
    summed = fs[...].reshape(ROWS, 2 * FEATURES)
    summed = jnp.where(c == 0, summed[:, :FEATURES], summed[:, FEATURES:])
    state = jnp.concatenate([state, jnp.zeros_like(state)], axis=0).T[:, :FEATURES]
    out_ref[...] = state + summed
    for copy in pending:
        copy.wait_send()
    for run in gathered:
        run.sent()
    wait(rc, rs_send.at[0])
    for p, (at, n, axis) in enumerate(PARTS):
        wait(rb0.at[:, :, :, pl.ds(at, n)], rs_send.at[1 + p])
        wait(rb1.at[pl.ds(1, 15), pl.ds(at, n)], rs_send.at[1 + p])
    wait(fs.at[c], rs_send.at[4])


def per_device(
    hidden_state, gain_attn, gain_ffn, w_qkv, w_out, w_gate, w_up, w_down, kv_cache, lengths, row_order
):
    parts = len(PARTS)
    vmem = pltpu.VMEM
    dma = pltpu.SemaphoreType.DMA
    scratch = [
        vmem((QKV, D), BF16), vmem((FEATURES, D), BF16), vmem((FF, D), BF16), vmem((FF, D), BF16),
        vmem((FF, D), BF16), vmem((1, CACHE, 2 * KVH * HD), BF16), dma((7,)), vmem((ROWS, FEATURES), F32),
        vmem((4, 4, 4, 2, FEATURES, ROWS), BF16), vmem((4, 4, 4, 2, 1, ROWS), F32),
        vmem((4, 4, 4, 2, FEATURES, ROWS), BF16), vmem((4, 4, 4, 2, 1, ROWS), F32),
        vmem((4, 4, 4, 2, QH, HD), BF16),
        *[vmem((ROWS // 4 * FOLD, HD), F32)] * 4, vmem((QH, ROWS, HD), BF16),
        vmem((16, 8, 1, HD), F32), vmem((8, 16, 1, HD), F32), vmem((16, 8, 1, HD), F32),
        vmem((4, 4, 4, 2, ROWS // 2, 128), BF16), vmem((4, 4, 4, ROWS // 2, 128), BF16),
        vmem((3, 4, 4, ROWS // 2, 128), BF16), vmem((16, ROWS // 2, 128), BF16),
        vmem((2, ROWS // 2, 128), F32),
        vmem((ROWS, FF), BF16), vmem((FF, ROWS), F32), vmem((FF, ROWS), F32),
    ]
    for send_count, count in ((parts, parts * 12), (1, 12), (parts, parts * 12), (1, 12), (parts, parts * 12),
                              (22, 22), (5, 20)):
        scratch += [dma((send_count,)), dma((count,))]
    in_vmem = pl.BlockSpec(memory_space=pltpu.VMEM)
    anywhere = pl.BlockSpec(memory_space=pl.ANY)
    return pl.pallas_call(
        kernel,
        out_shape=jax.ShapeDtypeStruct((ROWS, FEATURES), F32),
        in_specs=[anywhere] + [in_vmem] * 4 + [anywhere] * 6,
        out_specs=in_vmem,
        scratch_shapes=scratch,
        compiler_params=pltpu.CompilerParams(
            collective_id=0, has_side_effects=True, vmem_limit_bytes=56 * 1024 * 1024
        ),
    )(
        hidden_state, gain_attn.reshape(1, FEATURES), gain_ffn.reshape(1, FEATURES),
        lengths.reshape(1, ROWS), row_order.reshape(1, ROWS),
        w_qkv, w_out, w_gate, w_up, w_down, kv_cache,
    )


def solution(mesh):
    both = ("role", "grp")
    in_specs = (
        P(None, both), P(both), P(both), P(both, None), P(both, None), P(both, None),
        P(both, None), P(both, None), P(both, None, None), P(), P(),
    )
    return jax.shard_map(
        per_device, mesh=mesh, in_specs=in_specs, out_specs=P(None, both), check_vma=False
    )
```

time: 103 us -> 86.6 us (0.84)
  Pallas kernels: 99.8 us -> 83.3 us
    pallas_call x1, Pallas kernels: 99.8 us -> 83.3 us  [per_device(): pl.pallas_call(kernel, out_shape=jax.ShapeDtypeStruct((ROWS, FEATURES), F...]
where the time goes in v2:
time: 86.6 us; the launch traced here: 86.3 us
  Pallas kernels  83.3 us (96%)
  local copies, waits for them, and re-layouts  3.01 us (3%)
    pallas_call x1, Pallas kernels, per_device(): pl.pallas_call(kernel, out_shape=jax.ShapeDtypeStruct((ROWS, FEATURES), F...  83.3 us

profile of v2, /device:TPU:1, one launch (start us, length us, event | category | flops | bytes accessed | tf_op | source)
XLA Modules:
  0.0 86.3 jit_solution(13538246130555004075)
XLA Ops:
  0.0 1.5 %copy.12.hs_hbm = f32[128,64]{1,0:T(8,128)} copy(f32[128,64]{0,1:T(8,128)} %param.11) | data formatting | bytes 65536 | tf_op args[0]
  1.5 83.3 %shard_map.109 = f32[128,64]{1,0:T(8,128)} custom-call(f32[128,64]{1,0:T(8,128)} %copy.12.hs_hbm, f32[1,64]{1,0:T(1,128)} %bitcast.4, f32[1,64]{1,0:T(1,128)} %bitcast.5, s32[1,128]{1,0:T(1,128)} %bitcast.6, s32[1,128]{1,0:T(1,128)} %bitcast.7, bf16[72,8192]{1,0:T(8,128)(2,1)} %wqkv_hbm.1, bf16[64,8192]{1,0:T(8,128)(2,1)} %wout_hbm.1, ...), custom_call_target="tpu_custom_call" | custom-call | tf_op jit(solution)/shard_map/pallas_call | solution.py:415
  84.8 1.5 %copy.13 = f32[128,64]{0,1:T(8,128)} copy(f32[128,64]{1,0:T(8,128)} %shard_map.109) | data formatting | bytes 65536 | tf_op jit(solution)/shard_map/pallas_call | solution.py:415

commit v3 on v2

v3 whole, which is shorter than its diff:
```python
import jax
import jax.numpy as jnp
from jax import lax
from jax.experimental import pallas as pl
from jax.experimental.pallas import tpu as pltpu
from jax.sharding import PartitionSpec as P

F32 = jnp.float32
BF16 = jnp.bfloat16
D = 8192
QH = 64
KVH = 4
HD = 128
ROWS = 128
DEVICES = 128
FOLD = QH + 8
FEATURES = D // DEVICES
QKV = (QH + 2 * KVH) * HD // DEVICES
FF = 53248 // DEVICES
CACHE = 1024
EPS = 1e-05
AXES = "yab"
MESH = pl.DeviceIdType.MESH

PARTS = ((0, 32, "b"), (32, 16, "a"), (48, 16, "y"))
GATHER_SEMS = 15
OFFSETS = sorted(((i, j) for i in range(4) for j in range(4) if i or j),
                 key=lambda o: -sum(min(k, 4 - k) for k in o))


def iota(shape, dim):
    return lax.broadcasted_iota(jnp.int32, shape, dim)


def dot(a, b, ca=1, cb=0):
    return lax.dot_general(a, b, (((ca,), (cb,)), ((), ())), preferred_element_type=F32)


def kernel(
    hs_hbm, ga_hbm, gf_hbm, len_hbm, ord_hbm,
    wqkv_hbm, wout_hbm, wg_hbm, wu_hbm, wd_hbm, kv_hbm,
    out_ref,
    wqkv, wout, wg, wu, wd, kv, load_sem,
    ga_ref, gf_ref, len_ref, ord_ref,
    hs, xa, sa, xf, sf, xt, f0, f1, att, t_buf, r1, r2,
    pt, rc, rb0, rb1, fs,
    hid_ref, gate_ref, up_ref,
    xa_send, xa_recv, sa_send, sa_recv, xf_send, xf_recv, sf_send, sf_recv,
    xt_send, xt_recv, aa_send, aa_recv, rs_send, rs_recv,
):
    role = lax.axis_index("role")
    grp = lax.axis_index("grp")
    c = lax.rem(grp, 2)
    here = {
        "x": lax.rem(lax.div(grp, 2), 4),
        "z": lax.rem(lax.div(grp, 8), 4),
        "y": lax.div(grp, 32) * 2 + role,
    }
    first_core = c == 0
    coord = {
        "y": here["y"],
        "a": jnp.where(first_core, here["z"], here["x"]),
        "b": jnp.where(first_core, here["x"], here["z"]),
    }
    me = role * 64 + grp

    def place_of(axis, value):
        return lax.rem(value, 2) * 2 + lax.div(value, 2) if axis == "y" else value

    def chip(x, y, z, core):
        return (lax.rem(y, 2), lax.div(y, 2) * 32 + z * 8 + x * 2 + core)

    def device(at):
        x = jnp.where(first_core, at["b"], at["a"])
        z = jnp.where(first_core, at["a"], at["b"])
        return chip(x, at["y"], z, c)

    def turned(value, k):
        return lax.rem(value + k + 4, 4)

    def shifted(axis, k):
        return moved((axis,), (k,))

    def peer(axis, k):
        return device(shifted(axis, k))

    sibling = chip(here["x"], here["y"], here["z"], 1 - c)

    def index(at, full=""):
        return tuple(slice(None) if a in full else place_of(a, at[a]) for a in AXES)

    def plane_of(axis):
        return AXES.replace(axis, "")

    def moved(axes, offsets):
        return {**coord, **{a: turned(coord[a], k) for a, k in zip(axes, offsets)}}

    def wait(ref, sem):
        pltpu.make_async_copy(ref, ref, sem).wait()

    pending = []

    def send(src, dst, send_sem, recv_sem, target):
        copy = pltpu.make_async_remote_copy(
            src_ref=src, dst_ref=dst, send_sem=send_sem, recv_sem=recv_sem,
            device_id=target, device_id_type=MESH,
        )
        copy.start()
        pending.append(copy)
        return copy

    loads = []
    for i, (src, dst) in enumerate(
        ((hs_hbm, hs), (ga_hbm, ga_ref), (gf_hbm, gf_ref), (len_hbm, len_ref), (ord_hbm, ord_ref), (wqkv_hbm, wqkv),
         (kv_hbm, kv), (wout_hbm, wout), (wg_hbm, wg), (wu_hbm, wu), (wd_hbm, wd))
    ):
        load = pltpu.make_async_copy(src, dst, load_sem.at[i])
        load.start()
        loads.append(load)

    others = [sibling]
    for axis in AXES:
        others += [device(moved(plane_of(axis), o)) for o in OFFSETS if 0 not in o]
        others += [peer(axis, k) for k in (1, 2, 3)]
    for k in (1, 2, 3):
        others.append(chip(turned(here["x"], k), here["y"], here["z"], 1 - c))
    barrier = pltpu.get_barrier_semaphore()
    for other in others:
        pl.semaphore_signal(barrier, inc=1, device_id=other, device_id_type=MESH)

    def gain_column(ref):
        gain = jnp.broadcast_to(ref[...], (ROWS, FEATURES))
        return jnp.concatenate([gain, gain], axis=1).T[:FEATURES]

    own = index(coord)
    loads[0].wait()
    loads[1].wait()
    gain_a = gain_column(ga_ref)
    state = hs[...]
    xa[own + (c,)] = (state * gain_a).astype(BF16)
    sa[0] = jnp.sum(state * state, axis=0, keepdims=True)
    pl.semaphore_wait(barrier, len(others))

    class Gather:
        def __init__(self, buf, axis, tail, send_sem, recv_sem, base):
            self.buf, self.axis, self.tail = buf, axis, tail
            self.plane = plane_of(axis)
            self.send_sem, self.recv_sem, self.base = send_sem.at[base], recv_sem, base * GATHER_SEMS

        def at(self, where):
            return self.buf.at[where + (c,) + self.tail]

        def sem(self, stage, row):
            return self.recv_sem.at[self.base + stage * 4 + row]

        def row(self, k):
            return index(moved(self.plane[:1], (k,)), self.plane[1:])

        def push(self, ref, sem, target):
            pltpu.make_async_remote_copy(
                src_ref=ref, dst_ref=ref, send_sem=self.send_sem, recv_sem=sem,
                device_id=target, device_id_type=MESH,
            ).start()

        def spread(self, offset):
            sem = self.sem(0, (4 - offset[0]) % 4) if offset[0] else self.sem(3, offset[1] - 1)
            self.push(self.at(own), sem, device(moved(self.plane, offset)))

        def along(self, where, k):
            for j in (2, 1, 3):
                self.push(self.at(where), self.sem(1, j if self.axis == "y" else k), peer(self.axis, j))

        def forward_near(self, j):
            where = index(moved(self.plane, (0, -j)))
            wait(self.at(where), self.sem(3, j - 1))
            self.along(where, 0)

        def forward(self, k):
            where = self.row(k)
            wait(self.at(where), self.sem(0, k))
            self.along(where, k)

        def share(self, k):
            slab = index(moved("y", (k,)), "ab")
            if self.axis != "y":
                some = tuple(pl.ds(0, 3) if a == self.axis else w for a, w in zip(AXES, slab))
                wait(self.at(some), self.sem(1, k))
            elif k:
                wait(self.at(slab), self.sem(1, 4 - k))
            self.push(self.at(slab), self.sem(2, k), sibling)

        def finish(self, k):
            wait(self.buf.at[index(moved("y", (k,)), "ab") + (1 - c,) + self.tail], self.sem(2, k))

        def sent(self):
            blocks = self.buf.reshape(DEVICES, *self.buf.shape[4:])
            wait(blocks.at[(pl.ds(0, 127),) + self.tail], self.send_sem)

    gathered = []

    class Squares:
        def __init__(self, buf, send_sem, recv_sem):
            self.buf, self.send_sem, self.recv_sem = buf, send_sem, recv_sem

        def push(self, row, to, sem, target):
            pltpu.make_async_remote_copy(
                src_ref=self.buf.at[row], dst_ref=self.buf.at[to], send_sem=self.send_sem.at[0],
                recv_sem=self.recv_sem.at[sem], device_id=target, device_id_type=MESH,
            ).start()

        def start(self):
            self.push(0, 4, 0, sibling)

        def step(self, stage):
            if stage == 0:
                wait(self.buf.at[4], self.recv_sem.at[0])
                self.buf[1] = self.buf[0] + self.buf[4]
            else:
                total = self.added(stage)
                self.buf[stage + 1] = total
            for k in (2, 1, 3):
                self.push(stage + 1, 5 + stage * 3 + k - 1, stage + 1, peer("bay"[stage], k))

        def added(self, stage):
            first = 5 + (stage - 1) * 3
            wait(self.buf.at[pl.ds(first, 3)], self.recv_sem.at[stage])
            return self.buf[stage] + self.buf[first] + self.buf[first + 1] + self.buf[first + 2]

        def scale(self):
            return lax.rsqrt(self.added(3) * (1.0 / D) + EPS)

        def sent(self):
            wait(self.buf.at[pl.ds(0, 10)], self.send_sem.at[0])

    def gather(x, x_send, x_recv, on_slab, squares=None, beside=None):
        runs = []
        for p, (at, n, axis) in enumerate(PARTS):
            runs.append(Gather(x, axis, (pl.ds(at, n),), x_send, x_recv, p))
        gathered.extend(runs)
        if squares is not None:
            gathered.append(squares)
            squares.start()
        for run in runs:
            run.along(own, 0)
        for offset in OFFSETS:
            for run in runs:
                run.spread(offset)
        if squares is not None:
            squares.step(0)
        if beside is not None:
            beside()
        for j in (1, 3, 2):
            for run in runs:
                run.forward_near(j)
        if squares is not None:
            squares.step(1)
        for k in (1, 3, 2):
            for run in runs:
                run.forward(k)
        if squares is not None:
            squares.step(2)
        order = (0, 1, 3, 2)
        for run in runs:
            run.share(0)
        for i, k in enumerate(order):
            for run in runs:
                if i < 3:
                    run.share(order[i + 1])
            for run in runs:
                run.finish(k)
            on_slab(i, place_of("y", moved("y", (k,))["y"]))

    def block_at(x, y, i):
        i, core = divmod(i, 2)
        return x[(y, i // 4, i % 4, 0) if core == 0 else (y, i % 4, i // 4, 1)]

    def slab_of_features(x, y):
        return jnp.concatenate([block_at(x, y, i) for i in range(ROWS // 4)], axis=0)

    def slab_lanes(y):
        return pl.ds(pl.multiple_of(y * (D // 4), D // 4), D // 4)

    first_squares = Squares(sa, sa_send, sa_recv)
    local = {}

    def one_hots():
        for load in loads[2:5]:
            load.wait()
        order_row = ord_ref[...]
        by_seq = (iota((ROWS, ROWS), 0) == order_row).astype(F32)
        local["by_slot"] = by_seq.T.astype(BF16)
        lane = iota((1, ROWS), 1)
        my_seq = jnp.sum(jnp.where(lane == me, order_row, 0), axis=1, keepdims=True)
        local["my_len"] = jnp.sum(jnp.where(lane == my_seq, len_ref[...], 0), axis=1, keepdims=True)
        local["gain_f"] = gain_column(gf_ref)
        loads[5].wait()

    def project(i, y):
        term = dot(wqkv[:, slab_lanes(y)], slab_of_features(xa, y))
        local["proj"] = local["proj"] + term if i else term

    gather(xa, xa_send, xa_recv, project, first_squares, one_hots)
    by_slot, my_len = local["by_slot"], local["my_len"]
    proj = (local["proj"] * first_squares.scale()).astype(BF16)

    lane_of = lax.rem(me * QKV + iota((QKV, HD), 0), HD)
    place = (lane_of == iota((QKV, HD), 1)).astype(BF16)
    placed = dot(proj, place, 0, 0).astype(BF16)
    t_buf[...] = dot(by_slot, placed).reshape(16, 8, 1, HD)
    xc = here["x"] * 2 + c
    yz = place_of("y", here["y"]) * 4 + here["z"]
    first, second = [], []
    n = 0
    for kx in (2, 1, 3, 0):
        for kc in (1, 0):
            if kx or kc:
                x, core = turned(here["x"], kx), lax.rem(c + kc, 2)
                first.append(send(t_buf.at[:, x * 2 + core], r1.at[xc], aa_send.at[n], aa_recv.at[n],
                                  chip(x, here["y"], here["z"], core)))
                n += 1
    r1[xc] = t_buf[:, xc]
    for copy in first:
        copy.wait_recv()
    for o in OFFSETS:
        y, z = turned(here["y"], o[0]), turned(here["z"], o[1])
        second.append(send(r1.at[:, place_of("y", y) * 4 + z], r2.at[yz], aa_send.at[n], aa_recv.at[n],
                           chip(here["x"], y, z, c)))
        n += 1
    r2[yz] = r1[:, yz]
    for copy in second:
        copy.wait_recv()
    got = r2[...].reshape(DEVICES, HD)
    start = iota((DEVICES, HD), 0) * QKV
    late = iota((DEVICES, HD), 1) >= lax.rem(start, HD)
    heads = QH + 2 * KVH
    src_head = lax.div(iota((heads, DEVICES), 1) * QKV, HD)
    head = iota((heads, DEVICES), 0)
    qkv = dot((src_head == head).astype(BF16), jnp.where(late, got, 0.0).astype(BF16))
    qkv = qkv + dot((src_head + 1 == head).astype(BF16), jnp.where(late, 0.0, got).astype(BF16))

    loads[6].wait()
    groups = QH // KVH
    valid = iota((groups, CACHE), 1) < my_len
    outs = []
    for h in range(KVH):
        q = qkv[h * groups:(h + 1) * groups]
        k_new = qkv[QH + h:QH + h + 1]
        v_new = qkv[QH + KVH + h:QH + KVH + h + 1]
        keys = kv[0, :, h * HD:(h + 1) * HD]
        values = kv[0, :, (KVH + h) * HD:(KVH + h + 1) * HD]
        cached = jnp.where(valid, dot(q.astype(BF16), keys, 1, 1) * (1.0 / HD ** 0.5), -1e30)
        fresh = jnp.sum(q * k_new, axis=1, keepdims=True) * (1.0 / HD ** 0.5)
        top = jnp.maximum(jnp.max(cached, axis=1, keepdims=True), fresh)
        cached_w = jnp.where(valid, jnp.exp(cached - top), 0.0)
        fresh_w = jnp.exp(fresh - top)
        total = jnp.sum(cached_w, axis=1, keepdims=True) + fresh_w
        summed = dot(cached_w.astype(BF16), values) + fresh_w.astype(BF16).astype(F32) * v_new
        outs.append((summed / total).astype(BF16))
    xt[own + (c,)] = jnp.concatenate(outs, axis=0)

    def regroup(i, y):
        fold = (f0, f1)[i % 2]
        slots = ROWS // 4
        for j in range(slots):
            fold[j * FOLD:j * FOLD + QH] = block_at(xt, y, j).astype(F32)
        rows = pl.ds(pl.multiple_of(y * slots, slots), slots)
        for h in range(QH):
            att[h, rows] = fold[pl.ds(h, slots, stride=FOLD)].astype(BF16)

    gather(xt, xt_send, xt_recv, regroup)
    loads[7].wait()
    delta = jnp.zeros((FEATURES, ROWS), F32)
    for h in range(0, QH, 16):
        block = jnp.concatenate([att[i] for i in range(h, h + 16)], axis=1)
        delta = delta + dot(wout[:, h * HD:(h + 16) * HD], block, 1, 1)
    for _ in range(3):
        term = delta.astype(BF16)
        state = state + dot(term, by_slot)
        delta = delta - term.astype(F32)

    xf[own + (c,)] = (state * local["gain_f"]).astype(BF16)
    sf[0] = jnp.sum(state * state, axis=0, keepdims=True)
    second_squares = Squares(sf, sf_send, sf_recv)

    def expand(i, y):
        block = slab_of_features(xf, y)
        for w, acc in ((wg, gate_ref), (wu, up_ref)):
            term = dot(w[:, slab_lanes(y)], block)
            acc[...] = acc[...] + term if i else term

    def weights():
        loads[8].wait()
        loads[9].wait()

    gather(xf, xf_send, xf_recv, expand, second_squares, weights)
    scale = second_squares.scale()
    gate = gate_ref[...] * scale
    hidden = gate / (1.0 + jnp.exp(-gate)) * (up_ref[...] * scale)
    hid_ref[...] = hidden.astype(BF16).T

    loads[10].wait()
    half = ROWS // 2
    slabs = (2, 1, 3, 0)

    def push(src, dst, send_sem, recv_sem, target):
        pltpu.make_async_remote_copy(
            src_ref=src, dst_ref=dst, send_sem=send_sem, recv_sem=recv_sem,
            device_id=target, device_id_type=MESH,
        ).start()

    def slab_of(k):
        return place_of("y", moved("y", (k,))["y"])

    def down(k):
        y = slab_of(k)

        def chunk(z, carry):
            lanes = pl.ds(pl.multiple_of((y * 4 + z) * 512, 512), 512)
            term = dot(hid_ref[...], wd[:, lanes]).astype(BF16)
            for x in range(4):
                block = term[:, x * 128:(x + 1) * 128]
                pt[y, z, x, 0] = block[:half]
                pt[y, x, z, 1] = block[half:]
            return carry

        lax.fori_loop(0, 4, chunk, 0)
        push(pt.at[y, :, :, 1 - c], rc.at[y], rs_send.at[0], rs_recv.at[k], sibling)

    def along(k):
        y = slab_of(k)
        wait(rc.at[y], rs_recv.at[k])
        pt[y, :, :, c] = (pt[y, :, :, c].astype(F32) + rc[y].astype(F32)).astype(BF16)
        for p, (at, n, axis) in enumerate(PARTS):
            rows = pl.ds(at, n)
            if axis == "y":
                if k:
                    push(pt.at[y, :, :, c, rows], rb0.at[k - 1, :, :, rows],
                         rs_send.at[1 + p], rs_recv.at[4 + p * 5], peer("y", k))
                continue
            for j in (2, 1, 3):
                where = index({**shifted(axis, j), "y": moved("y", (k,))["y"]}, plane_of(axis)[1:])
                push(pt.at[where + (c, rows)], rb0.at[j - 1, y, :, rows],
                     rs_send.at[1 + p], rs_recv.at[4 + p * 5 + k], peer(axis, j))

    def across(p, line, where, sem, offsets):
        at, n, axis = PARTS[p]
        rows = pl.ds(at, n)
        wait(rb0.at[(slice(None),) + line + (rows,)], rs_recv.at[sem])
        value = pt[where + (c, rows)].astype(F32)
        for j in range(3):
            value = value + rb0[(j,) + line + (rows,)].astype(F32)
        pt[where + (c, rows)] = value.astype(BF16)
        for o in offsets:
            target = moved(plane_of(axis), o)
            push(pt.at[index(target) + (c, rows)], rb1.at[o[0] * 4 + o[1], rows],
                 rs_send.at[1 + p], rs_recv.at[4 + p * 5 + 4], device(target))

    down(slabs[0])
    for i, k in enumerate(slabs):
        if i < 3:
            down(slabs[i + 1])
        along(k)
    for k in slabs:
        for p, (at, n, axis) in enumerate(PARTS):
            if axis != "y":
                where = index(moved("y", (k,)), plane_of(axis)[1:])
                across(p, (slab_of(k), slice(None)), where, 4 + p * 5 + k, [o for o in OFFSETS if o[0] == k])
            elif k == 1:
                across(p, (slice(None),) * 2, index(coord, "ab"), 4 + p * 5, OFFSETS)
    for p, (at, n, axis) in enumerate(PARTS):
        rows = pl.ds(at, n)
        wait(rb1.at[pl.ds(1, 15), rows], rs_recv.at[4 + p * 5 + 4])
        value = pt[own + (c, rows)].astype(F32)
        for i in range(1, 16):
            value = value + rb1[i, rows].astype(F32)
        fs[c, rows] = value
    push(fs.at[c], fs.at[c], rs_send.at[4], rs_recv.at[19], sibling)
    wait(fs.at[1 - c], rs_recv.at[19])
    summed = fs[...].reshape(ROWS, 2 * FEATURES)
    summed = jnp.where(c == 0, summed[:, :FEATURES], summed[:, FEATURES:])
    out_ref[...] = state + jnp.concatenate([summed, jnp.zeros_like(summed)], axis=1).T[:FEATURES]
    for copy in pending:
        copy.wait_send()
    for run in gathered:
        run.sent()
    wait(rc, rs_send.at[0])
    for p, (at, n, axis) in enumerate(PARTS):
        wait(rb0.at[:, :, :, pl.ds(at, n)], rs_send.at[1 + p])
        wait(rb1.at[pl.ds(1, 15), pl.ds(at, n)], rs_send.at[1 + p])
    wait(fs.at[c], rs_send.at[4])


def per_device(
    hidden_state, gain_attn, gain_ffn, w_qkv, w_out, w_gate, w_up, w_down, kv_cache, lengths, row_order
):
    parts = len(PARTS)
    vmem = pltpu.VMEM
    dma = pltpu.SemaphoreType.DMA
    scratch = [
        vmem((QKV, D), BF16), vmem((FEATURES, D), BF16), vmem((FF, D), BF16), vmem((FF, D), BF16),
        vmem((FF, D), BF16), vmem((1, CACHE, 2 * KVH * HD), BF16), dma((11,)),
        vmem((1, FEATURES), F32), vmem((1, FEATURES), F32), vmem((1, ROWS), jnp.int32), vmem((1, ROWS), jnp.int32),
        vmem((FEATURES, ROWS), F32),
        vmem((4, 4, 4, 2, FEATURES, ROWS), BF16), vmem((14, 1, ROWS), F32),
        vmem((4, 4, 4, 2, FEATURES, ROWS), BF16), vmem((14, 1, ROWS), F32),
        vmem((4, 4, 4, 2, QH, HD), BF16),
        *[vmem((ROWS // 4 * FOLD, HD), F32)] * 2, vmem((QH, ROWS, HD), BF16),
        vmem((16, 8, 1, HD), F32), vmem((8, 16, 1, HD), F32), vmem((16, 8, 1, HD), F32),
        vmem((4, 4, 4, 2, ROWS // 2, 128), BF16), vmem((4, 4, 4, ROWS // 2, 128), BF16),
        vmem((3, 4, 4, ROWS // 2, 128), BF16), vmem((16, ROWS // 2, 128), BF16),
        vmem((2, ROWS // 2, 128), F32),
        vmem((ROWS, FF), BF16), vmem((FF, ROWS), F32), vmem((FF, ROWS), F32),
    ]
    for send_count, count in ((parts, parts * GATHER_SEMS), (1, 4), (parts, parts * GATHER_SEMS), (1, 4),
                              (parts, parts * GATHER_SEMS), (22, 22), (5, 20)):
        scratch += [dma((send_count,)), dma((count,))]
    in_vmem = pl.BlockSpec(memory_space=pltpu.VMEM)
    anywhere = pl.BlockSpec(memory_space=pl.ANY)
    out = pl.pallas_call(
        kernel,
        out_shape=jax.ShapeDtypeStruct((FEATURES, ROWS), F32),
        in_specs=[anywhere] * 11,
        out_specs=in_vmem,
        scratch_shapes=scratch,
        compiler_params=pltpu.CompilerParams(
            collective_id=0, has_side_effects=True, vmem_limit_bytes=56 * 1024 * 1024
        ),
    )(
        hidden_state.T, gain_attn.reshape(1, FEATURES), gain_ffn.reshape(1, FEATURES),
        lengths.reshape(1, ROWS), row_order.reshape(1, ROWS),
        w_qkv, w_out, w_gate, w_up, w_down, kv_cache,
    )
    return out.T


def solution(mesh):
    both = ("role", "grp")
    in_specs = (
        P(None, both), P(both), P(both), P(both, None), P(both, None), P(both, None),
        P(both, None), P(both, None), P(both, None, None), P(), P(),
    )
    return jax.shard_map(
        per_device, mesh=mesh, in_specs=in_specs, out_specs=P(None, both), check_vma=False
    )
```

time: 86.6 us -> 80.1 us (0.925)
  Pallas kernels: 83.3 us -> 78.5 us
  local copies, waits for them, and re-layouts: 3.01 us -> 1.38 us
    pallas_call x1, Pallas kernels: 83.3 us -> 78.5 us  [per_device(): pl.pallas_call(kernel, out_shape=jax.ShapeDtypeStruct((FEATURES, ROWS), F...]
    pallas_call x1 -> x0, local copies, waits for them, and re-layouts: 1.54 us -> none  [per_device(): pl.pallas_call(kernel, out_shape=jax.ShapeDtypeStruct((ROWS, FEATURES), F...]
where the time goes in v3:
time: 80.1 us; the launch traced here: 79.9 us
  Pallas kernels  78.5 us (98%)
  local copies, waits for them, and re-layouts  1.38 us (2%)
    pallas_call x1, Pallas kernels, per_device(): pl.pallas_call(kernel, out_shape=jax.ShapeDtypeStruct((FEATURES, ROWS), F...  78.5 us

profile of v3, /device:TPU:1, one launch (start us, length us, event | category | flops | bytes accessed | tf_op | source)
XLA Modules:
  0.0 79.9 jit_solution(16916634857786969511)
XLA Ops:
  0.0 78.5 %shard_map.109 = f32[64,128]{1,0:T(8,128)} custom-call(f32[64,128]{1,0:T(8,128)} %bitcast.7, f32[1,64]{1,0:T(1,128)} %bitcast.8, f32[1,64]{1,0:T(1,128)} %bitcast.9, s32[1,128]{1,0:T(1,128)} %bitcast.10, s32[1,128]{1,0:T(1,128)} %bitcast.11, bf16[72,8192]{1,0:T(8,128)(2,1)} %wqkv_hbm.1, bf16[64,8192]{1,0:T(8,128)(2,1)} %wout_hbm.1, ...), custom_call_target="tpu_custom_call" | custom-call | tf_op jit(solution)/shard_map/pallas_call | solution.py:519
  78.5 1.4 %copy.13 = f32[128,64]{0,1:T(8,128)} copy(f32[128,64]{0,1:T(8,128)} %bitcast.6) | data formatting | bytes 65536

commit v4 on v3

--- a/solution.py
+++ b/solution.py
@@ -24,8 +24,13 @@
 
 PARTS = ((0, 32, "b"), (32, 16, "a"), (48, 16, "y"))
 GATHER_SEMS = 15
-OFFSETS = sorted(((i, j) for i in range(4) for j in range(4) if i or j),
-                 key=lambda o: -sum(min(k, 4 - k) for k in o))
+
+
+def hops(*offsets):
+    return sum(min(k, 4 - k) for k in offsets)
+
+
+OFFSETS = sorted(((i, j) for i in range(4) for j in range(4) if i or j), key=lambda o: -hops(*o))
 
 
 def iota(shape, dim):
@@ -43,7 +48,7 @@
     wqkv, wout, wg, wu, wd, kv, load_sem,
     ga_ref, gf_ref, len_ref, ord_ref,
     hs, xa, sa, xf, sf, xt, f0, f1, att, t_buf, r1, r2,
-    pt, rc, rb0, rb1, fs,
+    pt, rc, rb0, rb1,
     hid_ref, gate_ref, up_ref,
     xa_send, xa_recv, sa_send, sa_recv, xf_send, xf_recv, sf_send, sf_recv,
     xt_send, xt_recv, aa_send, aa_recv, rs_send, rs_recv,
@@ -118,12 +123,17 @@
         load.start()
         loads.append(load)
 
-    others = [sibling]
+    others = {}
     for axis in AXES:
-        others += [device(moved(plane_of(axis), o)) for o in OFFSETS if 0 not in o]
-        others += [peer(axis, k) for k in (1, 2, 3)]
+        plane = plane_of(axis)
+        for o in OFFSETS:
+            if 0 not in o:
+                others.setdefault(hops(*o), []).append(device(moved(plane, o)))
+        for k in (1, 2, 3):
+            others.setdefault(hops(k), []).append(peer(axis, k))
     for k in (1, 2, 3):
-        others.append(chip(turned(here["x"], k), here["y"], here["z"], 1 - c))
+        others[hops(k)].append(chip(turned(here["x"], k), here["y"], here["z"], 1 - c))
+    others = [other for far in sorted(others, reverse=True) for other in others[far]] + [sibling]
     barrier = pltpu.get_barrier_semaphore()
     for other in others:
         pl.semaphore_signal(barrier, inc=1, device_id=other, device_id_type=MESH)
@@ -163,21 +173,17 @@
             ).start()
 
         def spread(self, offset):
-            sem = self.sem(0, (4 - offset[0]) % 4) if offset[0] else self.sem(3, offset[1] - 1)
+            sem = self.sem(0, (4 - offset[0]) % 4)
             self.push(self.at(own), sem, device(moved(self.plane, offset)))
 
         def along(self, where, k):
             for j in (2, 1, 3):
                 self.push(self.at(where), self.sem(1, j if self.axis == "y" else k), peer(self.axis, j))
 
-        def forward_near(self, j):
-            where = index(moved(self.plane, (0, -j)))
-            wait(self.at(where), self.sem(3, j - 1))
-            self.along(where, 0)
-
         def forward(self, k):
             where = self.row(k)
-            wait(self.at(where), self.sem(0, k))
+            come = where if k else tuple(pl.ds(0, 3) if a == self.plane[1] else w for a, w in zip(AXES, where))
+            wait(self.at(come), self.sem(0, k))
             self.along(where, k)
 
         def share(self, k):
@@ -208,67 +214,70 @@
                 recv_sem=self.recv_sem.at[sem], device_id=target, device_id_type=MESH,
             ).start()
 
-        def start(self):
-            self.push(0, 4, 0, sibling)
-
-        def step(self, stage):
-            if stage == 0:
-                wait(self.buf.at[4], self.recv_sem.at[0])
-                self.buf[1] = self.buf[0] + self.buf[4]
-            else:
-                total = self.added(stage)
-                self.buf[stage + 1] = total
+        def added(self, first, count, sem):
+            wait(self.buf.at[pl.ds(first + 1, count)], self.recv_sem.at[sem])
+            return jnp.sum(self.buf[first:first + count + 1].reshape(count + 1, ROWS), axis=0, keepdims=True)
+
+        def spread(self, o):
+            self.push(0, o[0] * 4 + o[1], 0, device(moved("ya", o)))
+
+        def along(self):
+            self.buf[17] = self.added(0, 15, 0)
             for k in (2, 1, 3):
-                self.push(stage + 1, 5 + stage * 3 + k - 1, stage + 1, peer("bay"[stage], k))
-
-        def added(self, stage):
-            first = 5 + (stage - 1) * 3
-            wait(self.buf.at[pl.ds(first, 3)], self.recv_sem.at[stage])
-            return self.buf[stage] + self.buf[first] + self.buf[first + 1] + self.buf[first + 2]
+                self.push(17, 17 + k, 1, peer("b", k))
+
+        def share(self):
+            self.buf[21] = self.added(17, 3, 1)
+            self.push(21, 22, 2, sibling)
 
         def scale(self):
-            return lax.rsqrt(self.added(3) * (1.0 / D) + EPS)
+            return lax.rsqrt(self.added(21, 1, 2) * (1.0 / D) + EPS)
 
         def sent(self):
-            wait(self.buf.at[pl.ds(0, 10)], self.send_sem.at[0])
-
-    def gather(x, x_send, x_recv, on_slab, squares=None, beside=None):
+            wait(self.buf.at[pl.ds(0, 19)], self.send_sem.at[0])
+
+    def gather(x, x_send, x_recv, on_slab, squares=None, beside=None, make=None):
         runs = []
         for p, (at, n, axis) in enumerate(PARTS):
             runs.append(Gather(x, axis, (pl.ds(at, n),), x_send, x_recv, p))
         gathered.extend(runs)
         if squares is not None:
             gathered.append(squares)
-            squares.start()
-        for run in runs:
-            run.along(own, 0)
-        for offset in OFFSETS:
-            for run in runs:
-                run.spread(offset)
-        if squares is not None:
-            squares.step(0)
+        if make is not None:
+            for run, (at, n, axis) in zip(runs, PARTS):
+                make(at, n)
+                for offset in OFFSETS:
+                    run.spread(offset)
+        else:
+            for offset in OFFSETS:
+                for run in runs:
+                    run.spread(offset)
+                if squares is not None:
+                    squares.spread(offset)
         if beside is not None:
             beside()
-        for j in (1, 3, 2):
-            for run in runs:
-                run.forward_near(j)
-        if squares is not None:
-            squares.step(1)
-        for k in (1, 3, 2):
+        for run in runs:
+            run.forward(0)
+        for k in (1, 3):
             for run in runs:
                 run.forward(k)
         if squares is not None:
-            squares.step(2)
+            squares.along()
+        for run in runs:
+            run.forward(2)
         order = (0, 1, 3, 2)
-        for run in runs:
-            run.share(0)
+        for k in order[:3]:
+            for run in runs:
+                run.share(k)
         for i, k in enumerate(order):
-            for run in runs:
-                if i < 3:
-                    run.share(order[i + 1])
+            if squares is not None and i == 0:
+                squares.share()
             for run in runs:
                 run.finish(k)
             on_slab(i, place_of("y", moved("y", (k,))["y"]))
+            if i == 0:
+                for run in runs:
+                    run.share(2)
 
     def block_at(x, y, i):
         i, core = divmod(i, 2)
@@ -341,8 +350,8 @@
     loads[6].wait()
     groups = QH // KVH
     valid = iota((groups, CACHE), 1) < my_len
-    outs = []
-    for h in range(KVH):
+
+    def attend(h):
         q = qkv[h * groups:(h + 1) * groups]
         k_new = qkv[QH + h:QH + h + 1]
         v_new = qkv[QH + KVH + h:QH + KVH + h + 1]
@@ -355,8 +364,7 @@
         fresh_w = jnp.exp(fresh - top)
         total = jnp.sum(cached_w, axis=1, keepdims=True) + fresh_w
         summed = dot(cached_w.astype(BF16), values) + fresh_w.astype(BF16).astype(F32) * v_new
-        outs.append((summed / total).astype(BF16))
-    xt[own + (c,)] = jnp.concatenate(outs, axis=0)
+        xt[own + (c, slice(h * groups, (h + 1) * groups))] = (summed / total).astype(BF16)
 
     def regroup(i, y):
         fold = (f0, f1)[i % 2]
@@ -367,13 +375,17 @@
         for h in range(QH):
             att[h, rows] = fold[pl.ds(h, slots, stride=FOLD)].astype(BF16)
 
-    gather(xt, xt_send, xt_recv, regroup)
+    def attend_rows(at, n):
+        for h in range(at // groups, (at + n) // groups):
+            attend(h)
+
+    gather(xt, xt_send, xt_recv, regroup, make=attend_rows)
     loads[7].wait()
     delta = jnp.zeros((FEATURES, ROWS), F32)
     for h in range(0, QH, 16):
         block = jnp.concatenate([att[i] for i in range(h, h + 16)], axis=1)
         delta = delta + dot(wout[:, h * HD:(h + 16) * HD], block, 1, 1)
-    for _ in range(3):
+    for _ in range(2):
         term = delta.astype(BF16)
         state = state + dot(term, by_slot)
         delta = delta - term.astype(F32)
@@ -396,10 +408,9 @@
     scale = second_squares.scale()
     gate = gate_ref[...] * scale
     hidden = gate / (1.0 + jnp.exp(-gate)) * (up_ref[...] * scale)
-    hid_ref[...] = hidden.astype(BF16).T
+    hid_ref[...] = hidden.astype(BF16)
 
     loads[10].wait()
-    half = ROWS // 2
     slabs = (2, 1, 3, 0)
 
     def push(src, dst, send_sem, recv_sem, target):
@@ -414,16 +425,12 @@
     def down(k):
         y = slab_of(k)
 
-        def chunk(z, carry):
-            lanes = pl.ds(pl.multiple_of((y * 4 + z) * 512, 512), 512)
-            term = dot(hid_ref[...], wd[:, lanes]).astype(BF16)
+        term = dot(wd[:, slab_lanes(y)], hid_ref[...], 0, 0).astype(BF16)
+        for z in range(4):
             for x in range(4):
-                block = term[:, x * 128:(x + 1) * 128]
-                pt[y, z, x, 0] = block[:half]
-                pt[y, x, z, 1] = block[half:]
-            return carry
-
-        lax.fori_loop(0, 4, chunk, 0)
+                block = term[(z * 4 + x) * 128:(z * 4 + x + 1) * 128]
+                pt[y, z, x, 0] = block[:FEATURES]
+                pt[y, x, z, 1] = block[FEATURES:]
         push(pt.at[y, :, :, 1 - c], rc.at[y], rs_send.at[0], rs_recv.at[k], sibling)
 
     def along(k):
@@ -473,12 +480,7 @@
         value = pt[own + (c, rows)].astype(F32)
         for i in range(1, 16):
             value = value + rb1[i, rows].astype(F32)
-        fs[c, rows] = value
-    push(fs.at[c], fs.at[c], rs_send.at[4], rs_recv.at[19], sibling)
-    wait(fs.at[1 - c], rs_recv.at[19])
-    summed = fs[...].reshape(ROWS, 2 * FEATURES)
-    summed = jnp.where(c == 0, summed[:, :FEATURES], summed[:, FEATURES:])
-    out_ref[...] = state + jnp.concatenate([summed, jnp.zeros_like(summed)], axis=1).T[:FEATURES]
+        out_ref[rows] = state[at:at + n] + value
     for copy in pending:
         copy.wait_send()
     for run in gathered:
@@ -487,7 +489,6 @@
     for p, (at, n, axis) in enumerate(PARTS):
         wait(rb0.at[:, :, :, pl.ds(at, n)], rs_send.at[1 + p])
         wait(rb1.at[pl.ds(1, 15), pl.ds(at, n)], rs_send.at[1 + p])
-    wait(fs.at[c], rs_send.at[4])
 
 
 def per_device(
@@ -501,18 +502,17 @@
         vmem((FF, D), BF16), vmem((1, CACHE, 2 * KVH * HD), BF16), dma((11,)),
         vmem((1, FEATURES), F32), vmem((1, FEATURES), F32), vmem((1, ROWS), jnp.int32), vmem((1, ROWS), jnp.int32),
         vmem((FEATURES, ROWS), F32),
-        vmem((4, 4, 4, 2, FEATURES, ROWS), BF16), vmem((14, 1, ROWS), F32),
-        vmem((4, 4, 4, 2, FEATURES, ROWS), BF16), vmem((14, 1, ROWS), F32),
+        vmem((4, 4, 4, 2, FEATURES, ROWS), BF16), vmem((23, 1, ROWS), F32),
+        vmem((4, 4, 4, 2, FEATURES, ROWS), BF16), vmem((23, 1, ROWS), F32),
         vmem((4, 4, 4, 2, QH, HD), BF16),
         *[vmem((ROWS // 4 * FOLD, HD), F32)] * 2, vmem((QH, ROWS, HD), BF16),
         vmem((16, 8, 1, HD), F32), vmem((8, 16, 1, HD), F32), vmem((16, 8, 1, HD), F32),
-        vmem((4, 4, 4, 2, ROWS // 2, 128), BF16), vmem((4, 4, 4, ROWS // 2, 128), BF16),
-        vmem((3, 4, 4, ROWS // 2, 128), BF16), vmem((16, ROWS // 2, 128), BF16),
-        vmem((2, ROWS // 2, 128), F32),
-        vmem((ROWS, FF), BF16), vmem((FF, ROWS), F32), vmem((FF, ROWS), F32),
+        vmem((4, 4, 4, 2, FEATURES, ROWS), BF16), vmem((4, 4, 4, FEATURES, ROWS), BF16),
+        vmem((3, 4, 4, FEATURES, ROWS), BF16), vmem((16, FEATURES, ROWS), BF16),
+        vmem((FF, ROWS), BF16), vmem((FF, ROWS), F32), vmem((FF, ROWS), F32),
     ]
     for send_count, count in ((parts, parts * GATHER_SEMS), (1, 4), (parts, parts * GATHER_SEMS), (1, 4),
-                              (parts, parts * GATHER_SEMS), (22, 22), (5, 20)):
+                              (parts, parts * GATHER_SEMS), (22, 22), (4, 19)):
         scratch += [dma((send_count,)), dma((count,))]
     in_vmem = pl.BlockSpec(memory_space=pltpu.VMEM)
     anywhere = pl.BlockSpec(memory_space=pl.ANY)

time: 80.1 us -> 77.1 us (0.963)
  Pallas kernels: 78.5 us -> 75.6 us
    pallas_call x1, Pallas kernels: 78.5 us -> 75.6 us  [per_device(): pl.pallas_call(kernel, out_shape=jax.ShapeDtypeStruct((FEATURES, ROWS), F...]
where the time goes in v4:
time: 77.1 us; the launch traced here: 76.9 us
  Pallas kernels  75.6 us (98%)
  local copies, waits for them, and re-layouts  1.38 us (2%)
    pallas_call x1, Pallas kernels, per_device(): pl.pallas_call(kernel, out_shape=jax.ShapeDtypeStruct((FEATURES, ROWS), F...  75.6 us

profile of v4, /device:TPU:1, one launch (start us, length us, event | category | flops | bytes accessed | tf_op | source)
XLA Modules:
  0.0 76.9 jit_solution(9503035715796231343)
XLA Ops:
  0.0 75.6 %shard_map.109 = f32[64,128]{1,0:T(8,128)} custom-call(f32[64,128]{1,0:T(8,128)} %bitcast.7, f32[1,64]{1,0:T(1,128)} %bitcast.8, f32[1,64]{1,0:T(1,128)} %bitcast.9, s32[1,128]{1,0:T(1,128)} %bitcast.10, s32[1,128]{1,0:T(1,128)} %bitcast.11, bf16[72,8192]{1,0:T(8,128)(2,1)} %wqkv_hbm.1, bf16[64,8192]{1,0:T(8,128)(2,1)} %wout_hbm.1, ...), custom_call_target="tpu_custom_call" | custom-call | tf_op jit(solution)/shard_map/pallas_call | solution.py:519
  75.6 1.4 %copy.13 = f32[128,64]{0,1:T(8,128)} copy(f32[128,64]{0,1:T(8,128)} %bitcast.6) | data formatting | bytes 65536

commit v5 on v4

--- a/solution.py
+++ b/solution.py
@@ -263,7 +263,7 @@
                 run.forward(k)
         if squares is not None:
             squares.along()
-        for run in runs:
+        for run in reversed(runs):
             run.forward(2)
         order = (0, 1, 3, 2)
         for k in order[:3]:
@@ -472,7 +472,7 @@
             if axis != "y":
                 where = index(moved("y", (k,)), plane_of(axis)[1:])
                 across(p, (slab_of(k), slice(None)), where, 4 + p * 5 + k, [o for o in OFFSETS if o[0] == k])
-            elif k == 1:
+            elif k == 3:
                 across(p, (slice(None),) * 2, index(coord, "ab"), 4 + p * 5, OFFSETS)
     for p, (at, n, axis) in enumerate(PARTS):
         rows = pl.ds(at, n)

time: 77.1 us -> 77.3 us (level)
  no operation moved by 1% of the time
where the time goes in v5:
time: 77.3 us; the launch traced here: 77.1 us
  Pallas kernels  75.7 us (98%)
  local copies, waits for them, and re-layouts  1.38 us (2%)
    pallas_call x1, Pallas kernels, per_device(): pl.pallas_call(kernel, out_shape=jax.ShapeDtypeStruct((FEATURES, ROWS), F...  75.7 us

profile of v5, /device:TPU:1, one launch (start us, length us, event | category | flops | bytes accessed | tf_op | source)
XLA Modules:
  0.0 77.1 jit_solution(6347863265364517256)
XLA Ops:
  0.0 75.7 %shard_map.109 = f32[64,128]{1,0:T(8,128)} custom-call(f32[64,128]{1,0:T(8,128)} %bitcast.7, f32[1,64]{1,0:T(1,128)} %bitcast.8, f32[1,64]{1,0:T(1,128)} %bitcast.9, s32[1,128]{1,0:T(1,128)} %bitcast.10, s32[1,128]{1,0:T(1,128)} %bitcast.11, bf16[72,8192]{1,0:T(8,128)(2,1)} %wqkv_hbm.1, bf16[64,8192]{1,0:T(8,128)(2,1)} %wout_hbm.1, ...), custom_call_target="tpu_custom_call" | custom-call | tf_op jit(solution)/shard_map/pallas_call | solution.py:519
  75.7 1.4 %copy.13 = f32[128,64]{0,1:T(8,128)} copy(f32[128,64]{0,1:T(8,128)} %bitcast.6) | data formatting | bytes 65536
